TPU v7x, 128 devices: a whole 4x4x4 slice. The times are simulated.
128 devices in a mesh: ctx: 16 (over x, z_lo, core), head: 8 (over y, z_hi).
Axes of the slice: x: 4, y: 4, z: 4 (z_hi: 2, z_lo: 2; z = z_hi * 2 + z_lo), core: 2. Of those that a mesh axis runs over, the one named last changes fastest.
Arguments:
- queries: bfloat16 [4096, 32, 256], P('ctx', 'head'), may hold values from -5 to 5
- cache_keys: bfloat16 [8192, 32, 256], P('ctx', 'head'), may hold values from -5 to 5
- cache_values: bfloat16 [8192, 32, 256], P('ctx', 'head'), may hold values from -6 to 6
- positions: int32 [4096], replicated, may hold values from 0 to 8191, as said below
- doc_spans: int32 [4096, 2], replicated, may hold values from 0 to 64, as said below
- lambdas: float32 [32], P('head'), may hold values from 0.2 to 0.8
- norm_gain: float32 [32, 256], P('head'), may hold values from 0.5 to 1.5
- out_weight: bfloat16 [8192, 8192], P('head'), may hold values from -0.0625 to 0.0625
Outputs:
- mixed: bfloat16 [4096, 8192], P(('ctx', 'head'))
Inputs may be any that keep to these rules, and one draw needn't show every extreme that they name: positions[q] >= 128 * doc_spans[q, 0], so every question sees at least one token. doc_spans[q, 0] < doc_spans[q, 1].
All inputs are finite; a program needn't handle non-finite values.
Results may differ from a plain program's by a relative error of at most 0.024.
Values may be sent and summed in bfloat16 or wider, within the bound.
A program may use at most 256 MiB of HBM per device.

v0:
```python
import jax
import jax.numpy as jnp
from jax import lax
from jax.sharding import PartitionSpec as P

BLK = 128


NEG_BIG = -1e30
LAMBDA_INIT = 0.8
EPSILON = 1e-05


def allowed_mask(positions, doc_spans, amount):
    tokens_at = jnp.arange(amount, dtype=jnp.int32)
    return (
        (tokens_at[None, :] <= positions[:, None])
        & (tokens_at[None, :] >= doc_spans[:, 0:1] * BLK)
        & (tokens_at[None, :] < doc_spans[:, 1:2] * BLK)
    )


def map_update(state, query_half, key_half, value_rows, allowed, factor):
    row_top, row_total, summed = state
    scores = (
        jnp.einsum("qhd,khd->qhk", query_half, key_half, preferred_element_type=jnp.float32)
        * factor
    )
    scores = jnp.where(allowed, scores, NEG_BIG)
    new_top = jnp.maximum(row_top, jnp.max(scores, axis=2))
    weights = jnp.where(allowed, jnp.exp(scores - new_top[:, :, None]), 0.0)
    new_total = jnp.sum(weights, axis=2)
    new_sum = jnp.einsum(
        "qhk,khv->qhv", weights.astype(jnp.bfloat16), value_rows, preferred_element_type=jnp.float32
    )
    return (new_top, new_total, new_sum)


def per_device(
    queries, cache_keys, cache_values, positions, doc_spans, lambdas, norm_gain, out_weight
):
    q_rows, heads_here, both_width = queries.shape
    half_width = both_width // 2
    factor = half_width ** (-0.5)
    value_width = cache_values.shape[2]
    first_half = queries[:, :, :half_width]
    second_half = queries[:, :, half_width:]
    ctx_idx = lax.axis_index("ctx")
    own_pos = lax.dynamic_slice_in_dim(positions, ctx_idx * q_rows, q_rows, 0)
    own_spans = lax.dynamic_slice_in_dim(doc_spans, ctx_idx * q_rows, q_rows, 0)
    start_top = jnp.full((q_rows, heads_here), NEG_BIG, jnp.float32)
    start_total = jnp.zeros((q_rows, heads_here), jnp.float32)
    start_sum = jnp.zeros((q_rows, heads_here, value_width), jnp.float32)
    totals = (start_top, start_total, start_sum, start_top, start_total, start_sum)
    block_keys = lax.all_gather(cache_keys, "ctx", axis=0, tiled=True)
    block_values = lax.all_gather(cache_values, "ctx", axis=0, tiled=True)
    allowed = allowed_mask(own_pos, own_spans, block_keys.shape[0])[:, None, :]
    state_one = map_update(
        totals[0:3], first_half, block_keys[:, :, :half_width], block_values, allowed, factor
    )
    state_two = map_update(
        totals[3:6], second_half, block_keys[:, :, half_width:], block_values, allowed, factor
    )
    finals = state_one + state_two
    attended = (
        finals[2] / finals[1][:, :, None]
        - lambdas[None, :, None] * finals[5] / finals[4][:, :, None]
    )
    mean_sq = jnp.mean(attended * attended, axis=-1, keepdims=True)
    normed = (
        attended * lax.rsqrt(mean_sq + EPSILON) * norm_gain[None] * (1.0 - LAMBDA_INIT)
    ).astype(jnp.bfloat16)
    flat_rows = normed.reshape(q_rows, heads_here * value_width)
    return lax.psum_scatter(
        jnp.dot(flat_rows, out_weight, preferred_element_type=jnp.float32).astype(jnp.bfloat16),
        "head",
        scatter_dimension=0,
        tiled=True,
    )


def solution(mesh):
    placed = (
        P("ctx", "head", None),
        P("ctx", "head", None),
        P("ctx", "head", None),
        P(),
        P(),
        P("head"),
        P("head", None),
        P("head", None),
    )
    return jax.shard_map(
        per_device, mesh=mesh, in_specs=placed, out_specs=P(("ctx", "head"), None), check_vma=False
    )
```

profile of v0, /device:TPU:0, one launch (start us, length us, event | category | flops | bytes accessed | tf_op | source)
XLA Modules:
  0.0 349.7 jit_solution(1625878224827225663)
XLA Ops:
  6.5 0.0 all-gather.3.cloned.1.call-start
  6.5 2.4 copy.9
  8.9 0.0 all-gather.3.cloned.1.call-update
  8.9 0.0 all-gather.5.cloned.1.call-start
  9.0 2.4 copy.11
  11.4 0.0 all-gather.5.cloned.1.call-update
  11.4 0.0 reduce-scatter.2.cloned.1.call-start
  11.4 0.8 dynamic_slice.6
  12.2 0.8 dynamic-slice_multiply_fusion.1
  13.0 1.2 fusion.44
  14.2 2.5 fusion.17
  16.7 86.5 %all-gather.3.cloned.1.call-done = bf16[8192,4,256]{2,0,1:T(8,128)(2,1)} async-done(((bf16[512,4,256]{2,0,1:T(8,128)(2,1)}), bf16[8192,4,256]{2,0,1:T(8,128)(2,1)}) %all-gather.3.cloned.1.call-update) | async-done | bytes 16777232 | tf_op jit(solution)/shard_map/all_gather | solution.py:55
  103.2 19.9 %fusion.14 = f32[4,8192,256]{2,1,0:T(8,128)} fusion(bf16[8192,4,256]{2,0,1:T(8,128)(2,1)} %all-gather.3.cloned.1.call-done, bf16[256,4,128]{2,1,0:T(4,128)(2,1)S(1)} %get-tuple-element.10), kind=kOutput, calls=%fused_computation.17 | convolution fusion | flops 2147483648 | bytes 42205184 | tf_op jit(solution)/shard_map/qhd,khd->qhk/dot_general | solution.py:26
  123.1 27.8 %fusion.1 = (f32[256,4]{0,1:T(4,128)S(1)}, f32[256,4]{0,1:T(4,128)S(1)}, f32[4,8192,256]{2,1,0:T(8,128)}) fusion(pred[256,8192]{0,1:T(8,128)(4,1)S(1)} %fusion.17, f32[4,8192,256]{2,1,0:T(8,128)} %fusion.14, bf16[256,4,128]{2,1,0:T(4,128)(2,1)S(1)} %get-tuple-element.9, bf16[8192,4,256]{2,0,1:T(8,128)(2,1)} %all-gather.3.cloned.1.call-done), kind=kOutput, calls=%fused_computation.5 | convolution fusion | flops 2197813248 | bytes 77864960 | tf_op jit(solution)/shard_map/qhd,khd->qhk/dot_general | solution.py:26
  150.8 25.8 %fusion.4 = (f32[256,4]{0,1:T(4,128)S(1)}, f32[256,4]{0,1:T(4,128)S(1)}) fusion(f32[4,8192,256]{2,1,0:T(8,128)} %get-tuple-element.13, f32[256,4]{0,1:T(4,128)S(1)} %get-tuple-element.16, pred[256,8192]{0,1:T(8,128)(4,1)S(1)} %fusion.17, f32[256,4]{0,1:T(4,128)S(1)} %get-tuple-element.17, f32[4,8192,256]{2,1,0:T(8,128)} %fusion.14), kind=kLoop, calls=%fused_computation.8 | loop fusion | flops 83884032 | bytes 69222400 | tf_op jit(solution)/shard_map/reduce_sum | solution.py:32
  176.6 20.6 %all-gather.5.cloned.1.call-done = bf16[8192,4,256]{0,2,1:T(8,128)(2,1)} async-done(((bf16[512,4,256]{0,2,1:T(8,128)(2,1)}), bf16[8192,4,256]{0,2,1:T(8,128)(2,1)}) %all-gather.5.cloned.1.call-update) | async-done | bytes 16777232 | tf_op jit(solution)/shard_map/all_gather | solution.py:56
  197.2 23.7 %fusion.33 = f32[256,4,256]{0,2,1:T(8,128)S(1)} fusion(bf16[8192,4,256]{0,2,1:T(8,128)(2,1)} %all-gather.5.cloned.1.call-done, f32[4,8192,256]{2,1,0:T(8,128)} %fusion.14, f32[256,4]{0,1:T(4,128)S(1)} %get-tuple-element.17, pred[256,8192]{0,1:T(8,128)(4,1)S(1)} %fusion.17, f32[256,4]{0,1:T(4,128)S(1)} %get-tuple-element.6), kind=kOutput, calls=%fused_computation.29 | convolution fusion | flops 4337172480 | bytes 53485568 | tf_op jit(solution)/shard_map/qhk,khv->qhv/dot_general | solution.py:33
  220.9 0.0 copy-start
  221.0 23.9 %multiply_reduce_fusion = (f32[256,4]{0,1:T(4,128)S(1)}, f32[256,4,256]{0,2,1:T(8,128)S(1)}) fusion(f32[256,4,256]{0,2,1:T(8,128)S(1)} %fusion.33, f32[256,4]{0,1:T(4,128)S(1)} %get-tuple-element.5, bf16[8192,4,256]{0,2,1:T(8,128)(2,1)} %all-gather.5.cloned.1.call-done, f32[4,8192,256]{2,1,0:T(8,128)} %get-tuple-element.13, ...), kind=kOutput, calls=%fused_computation.31 | convolution fusion | flops 4338220032 | bytes 54538256 | tf_op jit(solution)/shard_map/qhk,khv->qhv/dot_general | solution.py:33
  244.9 0.0 copy-done
  244.9 0.2 multiply_convert_fusion
  245.1 12.1 %convolution_convert_fusion = bf16[256,8192]{1,0:T(8,128)(2,1)} fusion(bf16[256,1024]{0,1:T(8,128)(2,1)S(1)} %bitcast.53, bf16[1024,8192]{1,0:T(8,128)(2,1)} %param.15), kind=kOutput, calls=%fused_computation.14 | convolution fusion | flops 4297064448 | bytes 21495808 | tf_op jit(solution)/shard_map/dot_general | solution.py:75
  257.2 0.0 reduce-scatter.2.cloned.1.call-update
  257.2 86.0 %reduce-scatter.2.cloned.1.call-done = bf16[32,8192]{1,0:T(8,128)(2,1)} async-done(((bf16[256,8192]{1,0:T(8,128)(2,1)}), bf16[32,8192]{1,0:T(8,128)(2,1)}) %reduce-scatter.2.cloned.1.call-update) | async-done | bytes 524304 | tf_op jit(solution)/shard_map/reduce_scatter | solution.py:74
  (4 shorter events, 0.0 us)
Async XLA Ops:
  6.5 96.7 %all-gather.3.cloned.1.call-start = ((), (), s32[]{:S(2)}) async-start(), calls=%async_computation.1 | async-start | bytes 17825792 | tf_op jit(solution)/shard_map/all_gather | solution.py:55
  8.9 188.3 %all-gather.5.cloned.1.call-start = ((), (), s32[]{:S(2)}) async-start(), calls=%async_computation.2 | async-start | bytes 17825792 | tf_op jit(solution)/shard_map/all_gather | solution.py:56
  11.4 331.8 %reduce-scatter.2.cloned.1.call-start = ((), (), s32[]{:S(2)}) async-start(), calls=%async_computation.3 | async-start | bytes 4718592 | tf_op jit(solution)/shard_map/reduce_scatter | solution.py:74
  197.2 23.7 %copy-start.1 = (f32[4]{0:T(128)S(1)}, f32[4]{0:T(128)}, u32[]{:S(2)}) copy-start(f32[4]{0:T(128)} %param.13) | copy-start | bytes 52
  220.9 24.0 %copy-start = (f32[4,256]{1,0:T(4,128)S(1)}, f32[4,256]{1,0:T(4,128)}, u32[]{:S(2)}) copy-start(f32[4,256]{1,0:T(4,128)} %param.14) | copy-start | bytes 12292
Sparse Core Ops, SparseCore 0:
  9.0 94.1 all-gather.2
  104.9 92.3 all-gather.4
  257.3 85.8 reduce-scatter.1
where the time goes:
time: 350 us
  waiting for transfers between devices  193 us (55%)
  matrix products  107 us (31%)
  other arithmetic  29.3 us (8%)
  between operations  13.2 us (4%)
  local copies, waits for them, and re-layouts  6.73 us (2%)
    all_gather x1, waiting for transfers between devices, per_device(): block_keys = lax.all_gather(cache_keys, 'ctx', axis=0, tiled=True)  86.5 us
    reduce_scatter x1, waiting for transfers between devices, per_device(): lax.psum_scatter(jnp.dot(flat_rows, out_weight, preferred_element_type=jn...  86 us
    dot_general x2, matrix products, map_update(): jnp.einsum('qhd,khd->qhk', query_half, key_half, preferred_element_type=j...  47.6 us
    dot_general x2, matrix products, map_update(): jnp.einsum('qhk,khv->qhv', weights.astype(jnp.bfloat16), value_rows, pref...  47.6 us
    reduce_sum x1, other arithmetic, map_update(): new_total = jnp.sum(weights, axis=2)  25.8 us
    all_gather x1, waiting for transfers between devices, per_device(): block_values = lax.all_gather(cache_values, 'ctx', axis=0, tiled=True)  20.6 us
    dot_general x1, matrix products, per_device(): jnp.dot(flat_rows, out_weight, preferred_element_type=jnp.float32)  12.1 us
  transfers between devices with their start and end apart: 3, of which 3 were waited for; matrix products, arithmetic and copies ran while one was open for 23% of the time, Pallas kernels for 0%

commit v1 on v0

v1 whole, which is shorter than its diff:
```python
import functools

import jax
import jax.numpy as jnp
from jax import lax
from jax.experimental import pallas as pl
from jax.experimental.pallas import tpu as pltpu
from jax.sharding import PartitionSpec as P

BLK = 128
NEG_BIG = -1e30
TOP_START = -1e29
LAMBDA_INIT = 0.8
EPSILON = 1e-05
LOG2_E = 1.4426950408889634
MESH = pl.DeviceIdType.MESH
PLANE = 4
RING = 4
PARTS = 4


def attention_kernel(
    q_ref, k_ref, v_ref, low_ref, high_ref, lam_ref, gain_ref, out_ref,
    q_all, k_all, v_all, v_turned, scores, sums, stats, pieces, landed, own_piece, turned_back, normed,
    q1_send, q1_recv, k_send, k_recv, v_send, v_recv, q2_send, q2_recv,
    st_send, st_recv, o_send, o_recv, n_send, n_recv, local_sem,
):
    ctx = lax.axis_index("ctx")
    head = lax.axis_index("head")
    x = ctx // PLANE
    j = lax.rem(ctx, PLANE)
    part_rows = q_all.shape[3]
    tile = PLANE * part_rows
    tokens = k_all.shape[0] * k_all.shape[1]
    value_width = v_all.shape[2]
    half = q_all.shape[4] // 2
    step = min(256, tokens)
    steps = tokens // step
    factor = (half ** -0.5) * LOG2_E
    n_tiles = PARTS * RING

    def plane_device(d):
        return (x * PLANE + lax.rem(j + d, PLANE), head)

    def ring_device(d):
        return (lax.rem(x + d, RING) * PLANE + j, head)

    barrier = pltpu.get_barrier_semaphore()
    for d in range(1, PLANE):
        pl.semaphore_signal(barrier, inc=1, device_id=plane_device(d), device_id_type=MESH)
    for d in range(1, RING):
        pl.semaphore_signal(barrier, inc=1, device_id=ring_device(d), device_id_type=MESH)
    pl.semaphore_wait(barrier, PLANE + RING - 2)

    def q1(d, dst):
        return pltpu.make_async_remote_copy(
            q_ref.at[lax.rem(j + d, PLANE)], q_all.at[:, x, dst], q1_send.at[d], q1_recv.at[d],
            device_id=plane_device(d), device_id_type=MESH)

    def k1(d, dst):
        return pltpu.make_async_remote_copy(
            k_ref.at[lax.rem(j + d, PLANE)], k_all.at[dst], k_send.at[d], k_recv.at[d],
            device_id=plane_device(d), device_id_type=MESH)

    def v1(d, dst):
        return pltpu.make_async_remote_copy(
            v_ref.at[lax.rem(j + d, PLANE)], v_all.at[dst], v_send.at[d], v_recv.at[d],
            device_id=plane_device(d), device_id_type=MESH)

    def q2(r, d, dst):
        return pltpu.make_async_remote_copy(
            q_all.at[r, x], q_all.at[r, dst], q2_send.at[r * RING + d], q2_recv.at[r * RING + d],
            device_id=ring_device(RING - d), device_id_type=MESH)

    def st(r, d, dst):
        return pltpu.make_async_remote_copy(
            stats.at[r, x], stats.at[r, dst], st_send.at[r * RING + d], st_recv.at[r * RING + d],
            device_id=ring_device(RING - d), device_id_type=MESH)

    def o1(r, d, dst):
        return pltpu.make_async_remote_copy(
            pieces.at[r, d], landed.at[r, dst], o_send.at[r * RING + d], o_recv.at[r * RING + d],
            device_id=ring_device(RING - d), device_id_type=MESH)

    def n1(r, d, dst):
        return pltpu.make_async_remote_copy(
            turned_back.at[r, lax.rem(j + d, PLANE)], normed.at[dst, r], n_send.at[r * PLANE + d], n_recv.at[r * PLANE + d],
            device_id=plane_device(d), device_id_type=MESH)

    def plane_source(d):
        return lax.rem(j + PLANE - d, PLANE)

    def ring_source(d):
        return lax.rem(x + d, RING)

    for d in range(1, PLANE):
        q1(d, j).start()
    for d in range(1, PLANE):
        k1(d, j).start()
        v1(d, j).start()
    own_copies = [
        pltpu.make_async_copy(q_ref.at[j], q_all.at[:, x, j], local_sem.at[0]),
        pltpu.make_async_copy(k_ref.at[j], k_all.at[j], local_sem.at[1]),
        pltpu.make_async_copy(v_ref.at[j], v_all.at[j], local_sem.at[2]),
    ]
    for copy in own_copies:
        copy.start()
    own_copies[0].wait()
    for d in range(1, PLANE):
        q1(d, plane_source(d)).wait_recv()
    for r in range(PARTS):
        for d in range(1, RING):
            q2(r, d, x).start()
    own_copies[1].wait()
    own_copies[2].wait()
    for d in range(1, PLANE):
        k1(d, plane_source(d)).wait_recv()
        v1(d, plane_source(d)).wait_recv()
    for source in range(PLANE):
        held = k_all.shape[1]
        v_turned[:, source * held:(source + 1) * held] = v_all[source].T

    def score_step(n, m, t, slot, top):
        r, plane = n // RING, lax.rem(x + lax.rem(n, RING), RING)
        query = q_all[r, plane, :, :, m * half:(m + 1) * half].reshape(tile, half)
        lanes = pl.ds(pl.multiple_of((r * RING + plane) * tile, tile), tile)
        low = low_ref[:, lanes] - x * tokens
        high = high_ref[:, lanes] - x * tokens
        held = k_all.shape[1]
        first = t * step
        if step <= held:
            key = k_all[first // held, first % held:first % held + step, m * half:(m + 1) * half]
        else:
            key = k_all[:, :, m * half:(m + 1) * half].reshape(tokens, half)[first:first + step]
        s = lax.dot_general(key, query, (((1,), (1,)), ((), ())), preferred_element_type=jnp.float32)
        at = lax.broadcasted_iota(jnp.int32, (step, tile), 0) + first
        s = jnp.where((at >= low) & (at < high), s, NEG_BIG)
        scores[slot, first:first + step, :] = s
        return jnp.maximum(top, jnp.max(s, axis=0, keepdims=True))

    def weight_step(t, slot, shift, total, summed):
        first = t * step
        w = jnp.exp2(scores[slot, first:first + step, :] * factor - shift)
        total = total + jnp.sum(w, axis=0, keepdims=True)
        part = jnp.dot(
            v_turned[:, first:first + step], w.astype(jnp.bfloat16), preferred_element_type=jnp.float32)
        return total, (part if summed is None else summed + part)

    def send_stats(r):
        for d in range(1, RING):
            st(r, d, x).start()

    def combine(r):
        for d in range(1, RING):
            st(r, d, ring_source(d)).wait_recv()
        lam = lam_ref[j]
        for d in (1, 3, 2, 0):
            plane = lax.rem(x + RING - d, RING)
            lanes = pl.ds(pl.multiple_of(plane * tile, tile), tile)
            shares = []
            for m in range(2):
                tops = [stats[r, s, 2 * m:2 * m + 1, lanes] for s in range(RING)]
                totals = [stats[r, s, 2 * m + 1:2 * m + 2, lanes] for s in range(RING)]
                top = functools.reduce(jnp.maximum, tops)
                total = sum(a * jnp.exp2((b - top) * factor) for a, b in zip(totals, tops))
                own_top = stats[r, x, 2 * m:2 * m + 1, lanes]
                shares.append(jnp.exp2((own_top - top) * factor) / total)
            piece = sums[r, plane, 0] * shares[0] - sums[r, plane, 1] * (shares[1] * lam)
            if d == 0:
                own_piece[r] = piece
            else:
                pieces[r, d] = piece.astype(jnp.bfloat16)
                o1(r, d, d).start()

    def finish(r):
        for d in range(1, RING):
            o1(r, d, d).wait_recv()
        attended = own_piece[r]
        for d in range(1, RING):
            attended = attended + landed[r, d].astype(jnp.float32)
        mean_sq = jnp.mean(attended * attended, axis=0, keepdims=True)
        result = attended * lax.rsqrt(mean_sq + EPSILON)
        result = result * gain_ref[j, :, 0:1] * (1.0 - LAMBDA_INIT)
        turned_back[r] = result.T.astype(jnp.bfloat16).reshape(PLANE, part_rows, value_width)
        for d in range(1, PLANE):
            n1(r, d, j).start()
        normed[j, r] = turned_back[r, j]

    first_top = jnp.full((1, tile), TOP_START, jnp.float32)
    top = first_top
    for t in range(steps):
        top = score_step(0, 0, t, 0, top)

    def body(n, top):
        r, d = n // RING, lax.rem(n, RING)
        plane = lax.rem(x + d, RING)
        later = jnp.minimum(n + 1, n_tiles - 1)
        later_r, later_d = later // RING, lax.rem(later, RING)

        @pl.when((n + 1 < n_tiles) & (later_d > 0))
        def _():
            q2(later_r, later_d, ring_source(later_d)).wait_recv()

        lanes = pl.ds(pl.multiple_of(plane * tile, tile), tile)
        for m in range(2):
            next_top = first_top
            total = jnp.zeros((1, tile), jnp.float32)
            summed = None
            shift = top * factor
            for t in range(steps):
                next_top = score_step(n if m == 0 else later, 1 - m, t, 1 - m, next_top)
                total, summed = weight_step(t, m, shift, total, summed)
            sums[r, plane, m] = summed
            stats[r, x, 2 * m:2 * m + 1, lanes] = top
            stats[r, x, 2 * m + 1:2 * m + 2, lanes] = total
            top = next_top

        @pl.when(d == RING - 1)
        def _():
            send_stats(r)

        @pl.when((d == 1) & (n >= RING))
        def _():
            combine(r - 1)

        @pl.when((d == 2) & (n >= 2 * RING))
        def _():
            finish(r - 2)

        return top

    lax.fori_loop(0, n_tiles, body, top)
    combine(PARTS - 1)
    finish(PARTS - 2)
    finish(PARTS - 1)

    def last_waits(r, carry):
        for d in range(1, PLANE):
            n1(r, d, plane_source(d)).wait_recv()
            n1(r, d, j).wait_send()
        for d in range(1, RING):
            q2(r, d, x).wait_send()
            st(r, d, x).wait_send()
            o1(r, d, d).wait_send()
        return carry

    lax.fori_loop(0, PARTS, last_waits, 0)
    for d in range(1, PLANE):
        q1(d, j).wait_send()
        k1(d, j).wait_send()
        v1(d, j).wait_send()
    for source in range(PLANE):
        out_ref[:, source * value_width:(source + 1) * value_width] = normed[source].reshape(
            PARTS * part_rows, value_width)


def attention(queries, keys, values, low, high, lambdas, gain):
    heads, parts, part_rows, width = queries.shape
    held, value_width = values.shape[1:]
    tile = PLANE * part_rows
    tokens = PLANE * held
    vmem = pl.BlockSpec(memory_space=pltpu.VMEM)
    hbm = pl.BlockSpec(memory_space=pl.ANY)
    bf16, f32 = jnp.bfloat16, jnp.float32
    dma = pltpu.SemaphoreType.DMA
    return pl.pallas_call(
        attention_kernel,
        out_shape=jax.ShapeDtypeStruct((parts * part_rows, heads * value_width), bf16),
        in_specs=[hbm, hbm, hbm, vmem, vmem, pl.BlockSpec(memory_space=pltpu.SMEM), vmem],
        out_specs=vmem,
        scratch_shapes=[
            pltpu.VMEM((PARTS, RING, PLANE, part_rows, width), bf16),
            pltpu.VMEM((PLANE, held, width), bf16),
            pltpu.VMEM((PLANE, held, value_width), bf16),
            pltpu.VMEM((value_width, tokens), bf16),
            pltpu.VMEM((2, tokens, tile), f32),
            pltpu.VMEM((PARTS, RING, 2, value_width, tile), f32),
            pltpu.VMEM((PARTS, RING, 8, RING * tile), f32),
            pltpu.VMEM((PARTS, RING, value_width, tile), bf16),
            pltpu.VMEM((PARTS, RING, value_width, tile), bf16),
            pltpu.VMEM((PARTS, value_width, tile), f32),
            pltpu.VMEM((PARTS, PLANE, part_rows, value_width), bf16),
            pltpu.VMEM((PLANE, PARTS, part_rows, value_width), bf16),
            dma((PLANE,)), dma((PLANE,)), dma((PLANE,)), dma((PLANE,)), dma((PLANE,)), dma((PLANE,)),
            dma((PARTS * RING,)), dma((PARTS * RING,)), dma((PARTS * RING,)), dma((PARTS * RING,)),
            dma((PARTS * RING,)), dma((PARTS * RING,)), dma((PARTS * PLANE,)), dma((PARTS * PLANE,)),
            dma((3,)),
        ],
        compiler_params=pltpu.CompilerParams(
            collective_id=0, has_side_effects=True, vmem_limit_bytes=56 * 1024 * 1024),
    )(queries, keys, values, low, high, lambdas, gain)


def per_device(
    queries, cache_keys, cache_values, positions, doc_spans, lambdas, norm_gain, out_weight
):
    q_rows, heads_here, both_width = queries.shape
    part_rows = q_rows // PARTS
    by_head = lambda a: jnp.transpose(a, (1, 0, 2))
    asked = by_head(queries).reshape(heads_here, PARTS, part_rows, both_width)
    ordered = lambda a: a.reshape(RING, PLANE, PARTS, part_rows).transpose(2, 0, 1, 3).reshape(1, -1)
    low = ordered(doc_spans[:, 0] * BLK)
    high = ordered(jnp.minimum(positions + 1, doc_spans[:, 1] * BLK))
    gain = jnp.broadcast_to(norm_gain[:, :, None], norm_gain.shape + (128,))
    flat_rows = attention(
        asked, by_head(cache_keys), by_head(cache_values), low, high, lambdas, gain)
    return lax.psum_scatter(
        jnp.dot(flat_rows, out_weight, preferred_element_type=jnp.float32).astype(jnp.bfloat16),
        "head",
        scatter_dimension=0,
        tiled=True,
    )


def solution(mesh):
    placed = (
        P("ctx", "head", None),
        P("ctx", "head", None),
        P("ctx", "head", None),
        P(),
        P(),
        P("head"),
        P("head", None),
        P("head", None),
    )
    return jax.shard_map(
        per_device, mesh=mesh, in_specs=placed, out_specs=P(("ctx", "head"), None), check_vma=False
    )
```

time: 350 us -> 206 us (0.59)
  waiting for transfers between devices: 193 us -> 86.8 us
  matrix products: 107 us -> 12.4 us
  Pallas kernels: 0 us -> 82.7 us
  other arithmetic: 29.3 us -> 1.62 us
    all_gather x2 -> x0, waiting for transfers between devices: 107 us -> none  [the longest x1 86.5 us: per_device(): block_keys = lax.all_gather(cache_keys, 'ctx', axis=0, tiled=True)]
    dot_general x4 -> x0, matrix products: 95.2 us -> none  [the longest x2 47.6 us: map_update(): jnp.einsum('qhd,khd->qhk', query_half, key_half, preferred_element_type=j...]
    pallas_call x0 -> x1, Pallas kernels: none -> 82.7 us  [attention(): pl.pallas_call(attention_kernel, out_shape=jax.ShapeDtypeStruct((parts *...]
    reduce_sum x1 -> x0, other arithmetic: 25.8 us -> none  [map_update(): new_total = jnp.sum(weights, axis=2)]
    transpose x0 -> x3, local copies, waits for them, and re-layouts: none -> 5.08 us  [the longest x2 5.07 us: per_device(): by_head = lambda a: jnp.transpose(a, (1, 0, 2))]
    unnamed x6 -> x0, local copies, waits for them, and re-layouts: 4.75 us -> none
  transfers between devices with their start and end apart: 3 -> 1, of which waited for: 3 -> 1; matrix products, arithmetic and copies ran while one was open for 23% -> 0% of each run, Pallas kernels for 0% -> 0%
where the time goes in v1:
time: 206 us; the launch traced here: 205 us
  waiting for transfers between devices  86.8 us (42%)
  Pallas kernels  82.7 us (40%)
  between operations  13.4 us (7%)
  matrix products  12.4 us (6%)
  local copies, waits for them, and re-layouts  8.33 us (4%)
    reduce_scatter x1, waiting for transfers between devices, per_device(): lax.psum_scatter(jnp.dot(flat_rows, out_weight, preferred_element_type=jn...  86.8 us
    pallas_call x1, Pallas kernels, attention(): pl.pallas_call(attention_kernel, out_shape=jax.ShapeDtypeStruct((parts *...  82.7 us
    dot_general x1, matrix products, per_device(): jnp.dot(flat_rows, out_weight, preferred_element_type=jnp.float32)  12.4 us
    transpose x2, local copies, waits for them, and re-layouts, per_device(): by_head = lambda a: jnp.transpose(a, (1, 0, 2))  5.07 us
  transfers between devices with their start and end apart: 1, of which 1 were waited for; matrix products, arithmetic and copies ran while one was open for 0% of the time, Pallas kernels for 0%

profile of v1, /device:TPU:0, one launch (start us, length us, event | category | flops | bytes accessed | tf_op | source)
XLA Modules:
  0.0 205.3 jit_solution(6845493870537991768)
XLA Ops:
  6.5 0.0 reduce-scatter.2.cloned.1.call-start
  6.5 0.9 slice_multiply_fusion
  7.4 0.7 add_minimum_fusion
  8.2 0.1 reshape.21
  8.3 0.7 reshape.22.high_ref
  9.0 0.1 mul.14
  9.1 0.7 reshape.20.low_ref
  9.8 1.9 copy.13
  11.7 3.2 %copy_bitcast_fusion = (bf16[4,512,256]{2,1,0:T(8,128)(2,1)}, bf16[4,512,256]{2,1,0:T(8,128)(2,1)}) fusion(bf16[512,4,256]{2,1,0:T(4,128)(2,1)} %param.10, bf16[512,4,256]{2,1,0:T(4,128)(2,1)} %param.9), kind=kLoop, calls=%fused_computation.1 | loop fusion | bytes 4194304 | tf_op jit(solution)/shard_map/transpose | solution.py:299
  14.8 1.7 broadcast_in_dim.2.gain_ref
  16.5 82.7 %shard_map.82 = bf16[256,1024]{1,0:T(8,128)(2,1)} custom-call(bf16[4,4,64,256]{3,2,1,0:T(8,128)(2,1)} %bitcast.13, bf16[4,512,256]{2,1,0:T(8,128)(2,1)} %get-tuple-element.8.k_ref, bf16[4,512,256]{2,1,0:T(8,128)(2,1)} %get-tuple-element.7.v_ref, s32[1,4096]{1,0:T(1,128)} %reshape.20.low_ref, s32[1,4096]{1,0:T(1,128)} %reshape.22.high_ref, f32[4]{0:T(128)} %lam_ref.1, ...), custom_call_target="tpu_custom_call" | custom-call | tf_op jit(solution)/shard_map/pallas_call | solution.py:266
  99.3 12.4 %convolution_convert_fusion = bf16[256,8192]{1,0:T(8,128)(2,1)} fusion(bf16[256,1024]{1,0:T(8,128)(2,1)} %shard_map.82, bf16[1024,8192]{1,0:T(8,128)(2,1)} %param.15), kind=kOutput, calls=%fused_computation | convolution fusion | flops 4297064448 | bytes 21495808 | tf_op jit(solution)/shard_map/dot_general | solution.py:308
  111.6 0.0 reduce-scatter.2.cloned.1.call-update
  111.7 86.8 %reduce-scatter.2.cloned.1.call-done = bf16[32,8192]{1,0:T(8,128)(2,1)} async-done(((bf16[256,8192]{1,0:T(8,128)(2,1)}), bf16[32,8192]{1,0:T(8,128)(2,1)}) %reduce-scatter.2.cloned.1.call-update) | async-done | bytes 524304 | tf_op jit(solution)/shard_map/reduce_scatter | solution.py:307
  (2 shorter events, 0.0 us)
Async XLA Ops:
  6.5 191.9 %reduce-scatter.2.cloned.1.call-start = ((), (), s32[]{:S(2)}) async-start(), calls=%async_computation.1 | async-start | bytes 4718592 | tf_op jit(solution)/shard_map/reduce_scatter | solution.py:307
Sparse Core Ops, SparseCore 0:
  111.8 86.6 reduce-scatter.1

commit v2 on v1

--- a/solution.py
+++ b/solution.py
@@ -16,19 +16,26 @@
 MESH = pl.DeviceIdType.MESH
 PLANE = 4
 RING = 4
+COLUMN = 4
+SIDES = 2
+WEIGHTS_AT = 10
 PARTS = 4
 
 
 def attention_kernel(
-    q_ref, k_ref, v_ref, low_ref, high_ref, lam_ref, gain_ref, out_ref,
+    q_ref, k_ref, v_ref, low_ref, high_ref, lam_ref, gain_ref, w_ref, out_ref,
     q_all, k_all, v_all, v_turned, scores, sums, stats, pieces, landed, own_piece, turned_back, normed,
+    w_all, a_out, a_in, b_out, b_in, a_mine, a2_out, a2_in, b2_out, b2_in, result,
     q1_send, q1_recv, k_send, k_recv, v_send, v_recv, q2_send, q2_recv,
     st_send, st_recv, o_send, o_recv, n_send, n_recv, local_sem,
+    a_send, a_recv, b_send, b_recv, a2_send, a2_recv, b2_send, b2_recv,
 ):
     ctx = lax.axis_index("ctx")
     head = lax.axis_index("head")
     x = ctx // PLANE
     j = lax.rem(ctx, PLANE)
+    y = head // SIDES
+    side = lax.rem(head, SIDES)
     part_rows = q_all.shape[3]
     tile = PLANE * part_rows
     tokens = k_all.shape[0] * k_all.shape[1]
@@ -38,19 +45,32 @@
     steps = tokens // step
     factor = (half ** -0.5) * LOG2_E
     n_tiles = PARTS * RING
+    share = part_rows // (COLUMN * SIDES)
+    columns = w_ref.shape[1]
+    area = columns // 2
+    fold = area // 2
+    stripe = min(512, fold)
 
     def plane_device(d):
         return (x * PLANE + lax.rem(j + d, PLANE), head)
 
     def ring_device(d):
         return (lax.rem(x + d, RING) * PLANE + j, head)
+
+    def column_device(d):
+        return (ctx, lax.rem(y + d, COLUMN) * SIDES + side)
+
+    other_side = (ctx, y * SIDES + 1 - side)
 
     barrier = pltpu.get_barrier_semaphore()
     for d in range(1, PLANE):
         pl.semaphore_signal(barrier, inc=1, device_id=plane_device(d), device_id_type=MESH)
     for d in range(1, RING):
         pl.semaphore_signal(barrier, inc=1, device_id=ring_device(d), device_id_type=MESH)
-    pl.semaphore_wait(barrier, PLANE + RING - 2)
+    for d in range(1, COLUMN):
+        pl.semaphore_signal(barrier, inc=1, device_id=column_device(d), device_id_type=MESH)
+    pl.semaphore_signal(barrier, inc=1, device_id=other_side, device_id_type=MESH)
+    pl.semaphore_wait(barrier, PLANE + RING + COLUMN - 2)
 
     def q1(d, dst):
         return pltpu.make_async_remote_copy(
@@ -86,6 +106,24 @@
         return pltpu.make_async_remote_copy(
             turned_back.at[r, lax.rem(j + d, PLANE)], normed.at[dst, r], n_send.at[r * PLANE + d], n_recv.at[r * PLANE + d],
             device_id=plane_device(d), device_id_type=MESH)
+
+    def a1(r, d):
+        return pltpu.make_async_remote_copy(
+            a_out.at[r, lax.rem(y + d, COLUMN)], a_in.at[r, d], a_send.at[r * COLUMN + d], a_recv.at[r * COLUMN + d],
+            device_id=column_device(d), device_id_type=MESH)
+
+    def a2(r):
+        return pltpu.make_async_remote_copy(
+            a2_out.at[r], a2_in.at[r], a2_send.at[r], a2_recv.at[r], device_id=other_side, device_id_type=MESH)
+
+    def b1(r):
+        return pltpu.make_async_remote_copy(
+            b_out.at[r, 1 - side], b_in.at[r], b_send.at[r], b_recv.at[r], device_id=other_side, device_id_type=MESH)
+
+    def b2(r, d):
+        return pltpu.make_async_remote_copy(
+            b2_out.at[r, lax.rem(y + d, COLUMN)], b2_in.at[r, d], b2_send.at[r * COLUMN + d], b2_recv.at[r * COLUMN + d],
+            device_id=column_device(d), device_id_type=MESH)
 
     def plane_source(d):
         return lax.rem(j + PLANE - d, PLANE)
@@ -105,6 +143,8 @@
     ]
     for copy in own_copies:
         copy.start()
+    weights_copy = pltpu.make_async_copy(w_ref, w_all, local_sem.at[3])
+    weights_copy.start()
     own_copies[0].wait()
     for d in range(1, PLANE):
         q1(d, plane_source(d)).wait_recv()
@@ -186,6 +226,101 @@
             n1(r, d, j).start()
         normed[j, r] = turned_back[r, j]
 
+    def project(r):
+        for d in range(1, PLANE):
+            n1(r, d, plane_source(d)).wait_recv()
+        rows = jnp.concatenate([normed[h, r] for h in range(PLANE)], axis=1)
+
+        def product(first):
+            return jnp.dot(rows, w_all[:, pl.ds(pl.multiple_of(first, stripe), stripe)], preferred_element_type=jnp.float32)
+
+        def b_stripe(i, carry):
+            at = pl.ds(pl.multiple_of(i * stripe, stripe), stripe)
+            got = product(area + i * stripe).astype(jnp.bfloat16)
+            for side_to in range(SIDES):
+                b_out[r, side_to, :, at] = got[side_to * COLUMN * share:(side_to + 1) * COLUMN * share]
+            return carry
+
+        def a_stripe(i, carry):
+            at = pl.ds(pl.multiple_of(i * stripe, stripe), stripe)
+            got = product(i * stripe)
+            for y_to in range(COLUMN):
+                a_out[r, y_to, :, at] = jnp.concatenate(
+                    [got[(s * COLUMN + y_to) * share:(s * COLUMN + y_to + 1) * share] for s in range(SIDES)], axis=0
+                ).astype(jnp.bfloat16)
+            return carry
+
+        lax.fori_loop(0, area // stripe, b_stripe, 0)
+        b1(r).start()
+        lax.fori_loop(0, area // stripe, a_stripe, 0)
+        for d in (1, 3, 2):
+            a1(r, d).start()
+
+    def add_first(r):
+        b1(r).wait_recv()
+
+        def b_stripe(i, carry):
+            halves = []
+            for k in range(2):
+                at = pl.ds(pl.multiple_of(k * fold + i * stripe, stripe), stripe)
+                halves.append(b_out[r, side, :, at].astype(jnp.float32) + b_in[r, :, at].astype(jnp.float32))
+            at = pl.ds(pl.multiple_of(i * stripe, stripe), stripe)
+            for y_to in range(COLUMN):
+                b2_out[r, y_to, :, at] = jnp.concatenate(
+                    [got[y_to * share:(y_to + 1) * share] for got in halves], axis=0).astype(jnp.bfloat16)
+            return carry
+
+        lax.fori_loop(0, fold // stripe, b_stripe, 0)
+        for d in (1, 3, 2):
+            b2(r, d).start()
+        for d in range(1, COLUMN):
+            a1(r, d).wait_recv()
+
+        def a_stripe(i, carry):
+            others = []
+            for k in range(2):
+                at = pl.ds(pl.multiple_of(k * fold + i * stripe, stripe), stripe)
+                got = a_out[r, y, :, at].astype(jnp.float32)
+                for d in range(1, COLUMN):
+                    got = got + a_in[r, d, :, at].astype(jnp.float32)
+                a_mine[r, :, at] = jnp.where(side == 0, got[:share], got[share:])
+                others.append(jnp.where(side == 0, got[share:], got[:share]))
+            at = pl.ds(pl.multiple_of(i * stripe, stripe), stripe)
+            a2_out[r, :, at] = jnp.concatenate(others, axis=0).astype(jnp.bfloat16)
+            return carry
+
+        lax.fori_loop(0, fold // stripe, a_stripe, 0)
+        a2(r).start()
+
+    def add_last(r):
+        for d in range(1, COLUMN):
+            b2(r, d).wait_recv()
+        a2(r).wait_recv()
+
+        def last_stripe(i, carry):
+            at = pl.ds(pl.multiple_of(i * stripe, stripe), stripe)
+            a_got = a2_in[r, :, at].astype(jnp.float32)
+            b_got = b2_out[r, y, :, at].astype(jnp.float32)
+            for d in range(1, COLUMN):
+                b_got = b_got + b2_in[r, d, :, at].astype(jnp.float32)
+            for k in range(2):
+                rows = slice(k * share, (k + 1) * share)
+                here = pl.ds(pl.multiple_of(k * fold + i * stripe, stripe), stripe)
+                result[r, :, here] = a_mine[r, :, here] + a_got[rows]
+                there = pl.ds(pl.multiple_of(area + k * fold + i * stripe, stripe), stripe)
+                result[r, :, there] = b_got[rows]
+            return carry
+
+        lax.fori_loop(0, fold // stripe, last_stripe, 0)
+
+    stages = ((send_stats, 3), (combine, 5), (finish, 10), (project, 12), (add_first, 17), (add_last, 20))
+
+    def run_stages(n):
+        for stage, lag in reversed(stages):
+            @pl.when((n >= lag) & (n < lag + PARTS * RING) & (lax.rem(n + RING * RING - lag, RING) == 0))
+            def _():
+                stage((n - lag) // RING)
+
     first_top = jnp.full((1, tile), TOP_START, jnp.float32)
     top = first_top
     for t in range(steps):
@@ -215,33 +350,33 @@
             stats[r, x, 2 * m + 1:2 * m + 2, lanes] = total
             top = next_top
 
-        @pl.when(d == RING - 1)
+        @pl.when(n == WEIGHTS_AT)
         def _():
-            send_stats(r)
-
-        @pl.when((d == 1) & (n >= RING))
-        def _():
-            combine(r - 1)
-
-        @pl.when((d == 2) & (n >= 2 * RING))
-        def _():
-            finish(r - 2)
-
+            weights_copy.wait()
+
+        run_stages(n)
         return top
 
     lax.fori_loop(0, n_tiles, body, top)
-    combine(PARTS - 1)
-    finish(PARTS - 2)
-    finish(PARTS - 1)
+
+    def tail(n, carry):
+        run_stages(n)
+        return carry
+
+    lax.fori_loop(n_tiles, n_tiles - RING + stages[-1][1] + 1, tail, 0)
 
     def last_waits(r, carry):
         for d in range(1, PLANE):
-            n1(r, d, plane_source(d)).wait_recv()
             n1(r, d, j).wait_send()
         for d in range(1, RING):
             q2(r, d, x).wait_send()
             st(r, d, x).wait_send()
             o1(r, d, d).wait_send()
+        for d in range(1, COLUMN):
+            a1(r, d).wait_send()
+            b2(r, d).wait_send()
+        a2(r).wait_send()
+        b1(r).wait_send()
         return carry
 
     lax.fori_loop(0, PARTS, last_waits, 0)
@@ -249,12 +384,12 @@
         q1(d, j).wait_send()
         k1(d, j).wait_send()
         v1(d, j).wait_send()
-    for source in range(PLANE):
-        out_ref[:, source * value_width:(source + 1) * value_width] = normed[source].reshape(
-            PARTS * part_rows, value_width)
-
-
-def attention(queries, keys, values, low, high, lambdas, gain):
+    for i in range(columns // stripe):
+        at = slice(i * stripe, (i + 1) * stripe)
+        out_ref[:, at] = jnp.concatenate([result[r, :, at] for r in range(PARTS)], axis=0).astype(jnp.bfloat16)
+
+
+def layer(queries, keys, values, low, high, lambdas, gain, weights):
     heads, parts, part_rows, width = queries.shape
     held, value_width = values.shape[1:]
     tile = PLANE * part_rows
@@ -262,11 +397,14 @@
     vmem = pl.BlockSpec(memory_space=pltpu.VMEM)
     hbm = pl.BlockSpec(memory_space=pl.ANY)
     bf16, f32 = jnp.bfloat16, jnp.float32
+    share = part_rows // (COLUMN * SIDES)
+    columns = weights.shape[1]
+    area = columns // 2
     dma = pltpu.SemaphoreType.DMA
     return pl.pallas_call(
         attention_kernel,
-        out_shape=jax.ShapeDtypeStruct((parts * part_rows, heads * value_width), bf16),
-        in_specs=[hbm, hbm, hbm, vmem, vmem, pl.BlockSpec(memory_space=pltpu.SMEM), vmem],
+        out_shape=jax.ShapeDtypeStruct((parts * share, columns), bf16),
+        in_specs=[hbm, hbm, hbm, vmem, vmem, pl.BlockSpec(memory_space=pltpu.SMEM), vmem, hbm],
         out_specs=vmem,
         scratch_shapes=[
             pltpu.VMEM((PARTS, RING, PLANE, part_rows, width), bf16),
@@ -281,14 +419,27 @@
             pltpu.VMEM((PARTS, value_width, tile), f32),
             pltpu.VMEM((PARTS, PLANE, part_rows, value_width), bf16),
             pltpu.VMEM((PLANE, PARTS, part_rows, value_width), bf16),
+            pltpu.VMEM(weights.shape, bf16),
+            pltpu.VMEM((PARTS, COLUMN, SIDES * share, area), bf16),
+            pltpu.VMEM((PARTS, COLUMN, SIDES * share, area), bf16),
+            pltpu.VMEM((PARTS, SIDES, COLUMN * share, area), bf16),
+            pltpu.VMEM((PARTS, COLUMN * share, area), bf16),
+            pltpu.VMEM((PARTS, share, area), f32),
+            pltpu.VMEM((PARTS, 2 * share, area // 2), bf16),
+            pltpu.VMEM((PARTS, 2 * share, area // 2), bf16),
+            pltpu.VMEM((PARTS, COLUMN, 2 * share, area // 2), bf16),
+            pltpu.VMEM((PARTS, COLUMN, 2 * share, area // 2), bf16),
+            pltpu.VMEM((PARTS, share, columns), f32),
             dma((PLANE,)), dma((PLANE,)), dma((PLANE,)), dma((PLANE,)), dma((PLANE,)), dma((PLANE,)),
             dma((PARTS * RING,)), dma((PARTS * RING,)), dma((PARTS * RING,)), dma((PARTS * RING,)),
             dma((PARTS * RING,)), dma((PARTS * RING,)), dma((PARTS * PLANE,)), dma((PARTS * PLANE,)),
-            dma((3,)),
+            dma((4,)),
+            dma((PARTS * COLUMN,)), dma((PARTS * COLUMN,)), dma((PARTS,)), dma((PARTS,)),
+            dma((PARTS,)), dma((PARTS,)), dma((PARTS * COLUMN,)), dma((PARTS * COLUMN,)),
         ],
         compiler_params=pltpu.CompilerParams(
-            collective_id=0, has_side_effects=True, vmem_limit_bytes=56 * 1024 * 1024),
-    )(queries, keys, values, low, high, lambdas, gain)
+            collective_id=0, has_side_effects=True, vmem_limit_bytes=60 * 1024 * 1024),
+    )(queries, keys, values, low, high, lambdas, gain, weights)
 
 
 def per_device(
@@ -296,20 +447,16 @@
 ):
     q_rows, heads_here, both_width = queries.shape
     part_rows = q_rows // PARTS
+    share = part_rows // (COLUMN * SIDES)
     by_head = lambda a: jnp.transpose(a, (1, 0, 2))
-    asked = by_head(queries).reshape(heads_here, PARTS, part_rows, both_width)
-    ordered = lambda a: a.reshape(RING, PLANE, PARTS, part_rows).transpose(2, 0, 1, 3).reshape(1, -1)
+    asked = queries.reshape(COLUMN, SIDES, PARTS, share, heads_here, both_width).transpose(4, 2, 1, 0, 3, 5)
+    asked = asked.reshape(heads_here, PARTS, part_rows, both_width)
+    ordered = lambda a: a.reshape(RING, PLANE, COLUMN, SIDES, PARTS, share).transpose(4, 0, 1, 3, 2, 5).reshape(1, -1)
     low = ordered(doc_spans[:, 0] * BLK)
     high = ordered(jnp.minimum(positions + 1, doc_spans[:, 1] * BLK))
     gain = jnp.broadcast_to(norm_gain[:, :, None], norm_gain.shape + (128,))
-    flat_rows = attention(
-        asked, by_head(cache_keys), by_head(cache_values), low, high, lambdas, gain)
-    return lax.psum_scatter(
-        jnp.dot(flat_rows, out_weight, preferred_element_type=jnp.float32).astype(jnp.bfloat16),
-        "head",
-        scatter_dimension=0,
-        tiled=True,
-    )
+    return layer(
+        asked, by_head(cache_keys), by_head(cache_values), low, high, lambdas, gain, out_weight)
 
 
 def solution(mesh):

time: 206 us -> 145 us (0.70)
  waiting for transfers between devices: 86.8 us -> 0 us
  Pallas kernels: 82.7 us -> 132 us
  between operations: 13.4 us -> 0.05 us
  matrix products: 12.4 us -> 0 us
  local copies, waits for them, and re-layouts: 8.33 us -> 11.2 us
    reduce_scatter x1 -> x0, waiting for transfers between devices: 86.8 us -> none  [per_device(): lax.psum_scatter(jnp.dot(flat_rows, out_weight, preferred_element_type=jn...]
    pallas_call x1, Pallas kernels: 82.7 us -> 132 us  [layer(): pl.pallas_call(attention_kernel, out_shape=jax.ShapeDtypeStruct((parts *...]
    dot_general x1 -> x0, matrix products: 12.4 us -> none  [per_device(): jnp.dot(flat_rows, out_weight, preferred_element_type=jnp.float32)]
    reshape x3 -> x4, local copies, waits for them, and re-layouts: 1.47 us -> 3.98 us  [the longest x3 2.05 us: per_device(): a.reshape(RING, PLANE, COLUMN, SIDES, PARTS, share)]
    transpose x2 -> x1, local copies, waits for them, and re-layouts: 5.07 us -> 3.17 us  [per_device(): by_head = lambda a: jnp.transpose(a, (1, 0, 2))]
  transfers between devices with their start and end apart: 1 -> 0, of which waited for: 1 -> 0; matrix products, arithmetic and copies ran while one was open for 0% -> 0% of each run, Pallas kernels for 0% -> 0%
where the time goes in v2:
time: 145 us; the launch traced here: 144 us
  Pallas kernels  132 us (91%)
  local copies, waits for them, and re-layouts  11.2 us (8%)
  other arithmetic  1.62 us (1%)
    pallas_call x1, Pallas kernels, layer(): pl.pallas_call(attention_kernel, out_shape=jax.ShapeDtypeStruct((parts *...  132 us
    transpose x1, local copies, waits for them, and re-layouts, per_device(): by_head = lambda a: jnp.transpose(a, (1, 0, 2))  3.17 us

profile of v2, /device:TPU:0, one launch (start us, length us, event | category | flops | bytes accessed | tf_op | source)
XLA Modules:
  0.0 144.4 jit_solution(7352069506214582917)
XLA Ops:
  0.0 0.9 slice_multiply_fusion
  0.9 0.7 add_minimum_fusion
  1.6 0.3 reshape.25
  2.0 0.1 copy.17
  2.1 0.9 reshape.26.high_ref
  2.9 0.3 mul.14
  3.3 0.1 copy.21
  3.3 0.9 reshape.24.low_ref
  4.2 1.9 %copy.13 = bf16[4,2,4,8,4,256]{5,3,0,1,2,4:T(8,128)(2,1)} copy(bf16[4,2,4,8,4,256]{5,4,3,2,1,0:T(4,128)(2,1)} %bitcast.16) | data formatting | bytes 1048576 | tf_op jit(solution)/shard_map/reshape | solution.py:452
  6.1 1.7 %broadcast_in_dim.2.gain_ref = f32[4,256,128]{2,1,0:T(8,128)} broadcast(f32[4,256]{1,0:T(4,128)} %param.14), dimensions={0,1} | broadcast | bytes 528384 | tf_op jit(solution)/shard_map/broadcast_in_dim | solution.py:457
  7.8 3.2 %copy_bitcast_fusion = (bf16[4,512,256]{2,1,0:T(8,128)(2,1)}, bf16[4,512,256]{2,1,0:T(8,128)(2,1)}) fusion(bf16[512,4,256]{2,1,0:T(4,128)(2,1)} %param.10, bf16[512,4,256]{2,1,0:T(4,128)(2,1)} %param.9), kind=kLoop, calls=%fused_computation | loop fusion | bytes 4194304 | tf_op jit(solution)/shard_map/transpose | solution.py:451
  11.0 131.6 %shard_map.82 = bf16[32,8192]{1,0:T(8,128)(2,1)} custom-call(bf16[4,4,64,256]{3,2,1,0:T(8,128)(2,1)} %bitcast.13, bf16[4,512,256]{2,1,0:T(8,128)(2,1)} %get-tuple-element.8.k_ref, bf16[4,512,256]{2,1,0:T(8,128)(2,1)} %get-tuple-element.7.v_ref, s32[1,4096]{1,0:T(1,128)} %reshape.24.low_ref, s32[1,4096]{1,0:T(1,128)} %reshape.26.high_ref, f32[4]{0:T(128)} %lam_ref.1, ...), custom_call_target="tpu_custom_call" | custom-call | tf_op jit(solution)/shard_map/pallas_call | solution.py:404
  142.6 1.9 %copy.23 = bf16[32,8192]{1,0:T(8,128)(2,1)} copy(bf16[32,8192]{1,0:T(8,128)(2,1)} %shard_map.82) | data formatting | bytes 1048576

commit v3 on v2

--- a/solution.py
+++ b/solution.py
@@ -18,12 +18,12 @@
 RING = 4
 COLUMN = 4
 SIDES = 2
-WEIGHTS_AT = 10
+HALVES = 2
 PARTS = 4
 
 
 def attention_kernel(
-    q_ref, k_ref, v_ref, low_ref, high_ref, lam_ref, gain_ref, w_ref, out_ref,
+    q_ref, k_ref, v_ref, span_ref, lam_ref, gain_ref, w_ref, out_ref,
     q_all, k_all, v_all, v_turned, scores, sums, stats, pieces, landed, own_piece, turned_back, normed,
     w_all, a_out, a_in, b_out, b_in, a_mine, a2_out, a2_in, b2_out, b2_in, result,
     q1_send, q1_recv, k_send, k_recv, v_send, v_recv, q2_send, q2_recv,
@@ -38,21 +38,29 @@
     side = lax.rem(head, SIDES)
     part_rows = q_all.shape[3]
     tile = PLANE * part_rows
-    tokens = k_all.shape[0] * k_all.shape[1]
+    held = k_all.shape[1]
+    tokens = PLANE * held
+    near = tokens // HALVES
     value_width = v_all.shape[2]
     half = q_all.shape[4] // 2
-    step = min(256, tokens)
-    steps = tokens // step
+    step = min(256, held)
+    steps = near // step
     factor = (half ** -0.5) * LOG2_E
-    n_tiles = PARTS * RING
+    half_tiles = PARTS * RING
+    n_tiles = HALVES * half_tiles
+    zp = j // 2
+    core = lax.rem(j, 2)
     share = part_rows // (COLUMN * SIDES)
     columns = w_ref.shape[1]
     area = columns // 2
     fold = area // 2
     stripe = min(512, fold)
 
-    def plane_device(d):
-        return (x * PLANE + lax.rem(j + d, PLANE), head)
+    def partner(k):
+        return (2 * zp + 1 - core, 2 * (1 - zp) + core, PLANE - 1 - j)[k - 1]
+
+    def plane_device(k):
+        return (x * PLANE + partner(k), head)
 
     def ring_device(d):
         return (lax.rem(x + d, RING) * PLANE + j, head)
@@ -74,17 +82,17 @@
 
     def q1(d, dst):
         return pltpu.make_async_remote_copy(
-            q_ref.at[lax.rem(j + d, PLANE)], q_all.at[:, x, dst], q1_send.at[d], q1_recv.at[d],
+            q_ref.at[partner(d)], q_all.at[:, x, dst], q1_send.at[d], q1_recv.at[d],
             device_id=plane_device(d), device_id_type=MESH)
 
     def k1(d, dst):
         return pltpu.make_async_remote_copy(
-            k_ref.at[lax.rem(j + d, PLANE)], k_all.at[dst], k_send.at[d], k_recv.at[d],
+            k_ref.at[partner(d)], k_all.at[dst], k_send.at[d], k_recv.at[d],
             device_id=plane_device(d), device_id_type=MESH)
 
     def v1(d, dst):
         return pltpu.make_async_remote_copy(
-            v_ref.at[lax.rem(j + d, PLANE)], v_all.at[dst], v_send.at[d], v_recv.at[d],
+            v_ref.at[partner(d)], v_all.at[dst], v_send.at[d], v_recv.at[d],
             device_id=plane_device(d), device_id_type=MESH)
 
     def q2(r, d, dst):
@@ -104,7 +112,7 @@
 
     def n1(r, d, dst):
         return pltpu.make_async_remote_copy(
-            turned_back.at[r, lax.rem(j + d, PLANE)], normed.at[dst, r], n_send.at[r * PLANE + d], n_recv.at[r * PLANE + d],
+            turned_back.at[r, partner(d)], normed.at[dst, r], n_send.at[r * PLANE + d], n_recv.at[r * PLANE + d],
             device_id=plane_device(d), device_id_type=MESH)
 
     def a1(r, d):
@@ -124,9 +132,6 @@
         return pltpu.make_async_remote_copy(
             b2_out.at[r, lax.rem(y + d, COLUMN)], b2_in.at[r, d], b2_send.at[r * COLUMN + d], b2_recv.at[r * COLUMN + d],
             device_id=column_device(d), device_id_type=MESH)
-
-    def plane_source(d):
-        return lax.rem(j + PLANE - d, PLANE)
 
     def ring_source(d):
         return lax.rem(x + d, RING)
@@ -145,45 +150,57 @@
         copy.start()
     weights_copy = pltpu.make_async_copy(w_ref, w_all, local_sem.at[3])
     weights_copy.start()
+    def clear(i, carry):
+        r, plane = i // RING, lax.rem(i, RING)
+        sums[r, plane] = jnp.zeros(sums.shape[2:], jnp.float32)
+        lanes = pl.ds(pl.multiple_of(plane * tile, tile), tile)
+        for m in range(2):
+            stats[r, x, 2 * m:2 * m + 1, lanes] = jnp.full((1, tile), TOP_START, jnp.float32)
+            stats[r, x, 2 * m + 1:2 * m + 2, lanes] = jnp.zeros((1, tile), jnp.float32)
+        return carry
+
+    lax.fori_loop(0, half_tiles, clear, 0)
     own_copies[0].wait()
     for d in range(1, PLANE):
-        q1(d, plane_source(d)).wait_recv()
+        q1(d, partner(d)).wait_recv()
     for r in range(PARTS):
-        for d in range(1, RING):
+        for d in (1, 3, 2):
             q2(r, d, x).start()
     own_copies[1].wait()
     own_copies[2].wait()
-    for d in range(1, PLANE):
-        k1(d, plane_source(d)).wait_recv()
-        v1(d, plane_source(d)).wait_recv()
-    for source in range(PLANE):
-        held = k_all.shape[1]
-        v_turned[:, source * held:(source + 1) * held] = v_all[source].T
+    k1(1, partner(1)).wait_recv()
+    v1(1, partner(1)).wait_recv()
+    for source in (j, partner(1)):
+        v_turned[source] = v_all[source].T
+
+    def place(n):
+        late = n // half_tiles
+        at = lax.rem(n, half_tiles)
+        return 2 * (zp + late - 2 * zp * late), at // RING, lax.rem(x + lax.rem(at, RING), RING)
 
     def score_step(n, m, t, slot, top):
-        r, plane = n // RING, lax.rem(x + lax.rem(n, RING), RING)
+        source, r, plane = place(n)
         query = q_all[r, plane, :, :, m * half:(m + 1) * half].reshape(tile, half)
         lanes = pl.ds(pl.multiple_of((r * RING + plane) * tile, tile), tile)
-        low = low_ref[:, lanes] - x * tokens
-        high = high_ref[:, lanes] - x * tokens
-        held = k_all.shape[1]
+        base = x * tokens + source * held
+        low = span_ref[0:1, lanes] - base
+        high = span_ref[1:2, lanes] - base
         first = t * step
-        if step <= held:
-            key = k_all[first // held, first % held:first % held + step, m * half:(m + 1) * half]
-        else:
-            key = k_all[:, :, m * half:(m + 1) * half].reshape(tokens, half)[first:first + step]
+        key = k_all[source + first // held, first % held:first % held + step, m * half:(m + 1) * half]
         s = lax.dot_general(key, query, (((1,), (1,)), ((), ())), preferred_element_type=jnp.float32)
         at = lax.broadcasted_iota(jnp.int32, (step, tile), 0) + first
         s = jnp.where((at >= low) & (at < high), s, NEG_BIG)
         scores[slot, first:first + step, :] = s
         return jnp.maximum(top, jnp.max(s, axis=0, keepdims=True))
 
-    def weight_step(t, slot, shift, total, summed):
+    def weight_step(n, t, slot, shift, total, summed):
+        source, _, _ = place(n)
         first = t * step
         w = jnp.exp2(scores[slot, first:first + step, :] * factor - shift)
         total = total + jnp.sum(w, axis=0, keepdims=True)
         part = jnp.dot(
-            v_turned[:, first:first + step], w.astype(jnp.bfloat16), preferred_element_type=jnp.float32)
+            v_turned[source + first // held, :, first % held:first % held + step], w.astype(jnp.bfloat16),
+            preferred_element_type=jnp.float32)
         return total, (part if summed is None else summed + part)
 
     def send_stats(r):
@@ -219,16 +236,16 @@
         for d in range(1, RING):
             attended = attended + landed[r, d].astype(jnp.float32)
         mean_sq = jnp.mean(attended * attended, axis=0, keepdims=True)
-        result = attended * lax.rsqrt(mean_sq + EPSILON)
-        result = result * gain_ref[j, :, 0:1] * (1.0 - LAMBDA_INIT)
-        turned_back[r] = result.T.astype(jnp.bfloat16).reshape(PLANE, part_rows, value_width)
+        turned = (attended * lax.rsqrt(mean_sq + EPSILON)).T
+        turned = turned * gain_ref[pl.ds(j, 1), :] * (1.0 - LAMBDA_INIT)
+        turned_back[r] = turned.astype(jnp.bfloat16).reshape(PLANE, part_rows, value_width)
         for d in range(1, PLANE):
             n1(r, d, j).start()
         normed[j, r] = turned_back[r, j]
 
     def project(r):
         for d in range(1, PLANE):
-            n1(r, d, plane_source(d)).wait_recv()
+            n1(r, d, partner(d)).wait_recv()
         rows = jnp.concatenate([normed[h, r] for h in range(PLANE)], axis=1)
 
         def product(first):
@@ -313,46 +330,54 @@
 
         lax.fori_loop(0, fold // stripe, last_stripe, 0)
 
-    stages = ((send_stats, 3), (combine, 5), (finish, 10), (project, 12), (add_first, 17), (add_last, 20))
+    stages = ((send_stats, 19), (combine, 23), (finish, 32), (project, 34), (add_first, 45), (add_last, 53))
 
     def run_stages(n):
         for stage, lag in reversed(stages):
-            @pl.when((n >= lag) & (n < lag + PARTS * RING) & (lax.rem(n + RING * RING - lag, RING) == 0))
+            @pl.when((n >= lag) & (n < lag + PARTS * RING) & (lax.rem(n + 16 * RING - lag, RING) == 0))
             def _():
                 stage((n - lag) // RING)
 
-    first_top = jnp.full((1, tile), TOP_START, jnp.float32)
-    top = first_top
+    def start_top(n, m):
+        _, r, plane = place(n)
+        return stats[r, x, 2 * m:2 * m + 1, pl.ds(pl.multiple_of(plane * tile, tile), tile)]
+
+    top = start_top(0, 0)
     for t in range(steps):
         top = score_step(0, 0, t, 0, top)
 
     def body(n, top):
-        r, d = n // RING, lax.rem(n, RING)
-        plane = lax.rem(x + d, RING)
+        _, r, plane = place(n)
         later = jnp.minimum(n + 1, n_tiles - 1)
-        later_r, later_d = later // RING, lax.rem(later, RING)
-
-        @pl.when((n + 1 < n_tiles) & (later_d > 0))
+        later_d = lax.rem(later, RING)
+
+        @pl.when((n + 1 < half_tiles) & (later_d > 0))
         def _():
-            q2(later_r, later_d, ring_source(later_d)).wait_recv()
+            q2(later // RING, later_d, ring_source(later_d)).wait_recv()
+
+        @pl.when(n + 1 == half_tiles)
+        def _():
+            for d in (2, 3):
+                k1(d, partner(d)).wait_recv()
+                v1(d, partner(d)).wait_recv()
+                v_turned[partner(d)] = v_all[partner(d)].T
+            weights_copy.wait()
 
         lanes = pl.ds(pl.multiple_of(plane * tile, tile), tile)
         for m in range(2):
-            next_top = first_top
+            following = n if m == 0 else later
+            next_top = start_top(following, 1 - m)
             total = jnp.zeros((1, tile), jnp.float32)
             summed = None
             shift = top * factor
             for t in range(steps):
-                next_top = score_step(n if m == 0 else later, 1 - m, t, 1 - m, next_top)
-                total, summed = weight_step(t, m, shift, total, summed)
-            sums[r, plane, m] = summed
+                next_top = score_step(following, 1 - m, t, 1 - m, next_top)
+                total, summed = weight_step(n, t, m, shift, total, summed)
+            kept = jnp.exp2((stats[r, x, 2 * m:2 * m + 1, lanes] - top) * factor)
+            sums[r, plane, m] = sums[r, plane, m] * kept + summed
             stats[r, x, 2 * m:2 * m + 1, lanes] = top
-            stats[r, x, 2 * m + 1:2 * m + 2, lanes] = total
+            stats[r, x, 2 * m + 1:2 * m + 2, lanes] = stats[r, x, 2 * m + 1:2 * m + 2, lanes] * kept + total
             top = next_top
-
-        @pl.when(n == WEIGHTS_AT)
-        def _():
-            weights_copy.wait()
 
         run_stages(n)
         return top
@@ -363,7 +388,7 @@
         run_stages(n)
         return carry
 
-    lax.fori_loop(n_tiles, n_tiles - RING + stages[-1][1] + 1, tail, 0)
+    lax.fori_loop(n_tiles, stages[-1][1] + PARTS * RING, tail, 0)
 
     def last_waits(r, carry):
         for d in range(1, PLANE):
@@ -389,7 +414,7 @@
         out_ref[:, at] = jnp.concatenate([result[r, :, at] for r in range(PARTS)], axis=0).astype(jnp.bfloat16)
 
 
-def layer(queries, keys, values, low, high, lambdas, gain, weights):
+def layer(queries, keys, values, spans, lambdas, gain, weights):
     heads, parts, part_rows, width = queries.shape
     held, value_width = values.shape[1:]
     tile = PLANE * part_rows
@@ -404,14 +429,14 @@
     return pl.pallas_call(
         attention_kernel,
         out_shape=jax.ShapeDtypeStruct((parts * share, columns), bf16),
-        in_specs=[hbm, hbm, hbm, vmem, vmem, pl.BlockSpec(memory_space=pltpu.SMEM), vmem, hbm],
+        in_specs=[hbm, hbm, hbm, vmem, pl.BlockSpec(memory_space=pltpu.SMEM), vmem, hbm],
         out_specs=vmem,
         scratch_shapes=[
             pltpu.VMEM((PARTS, RING, PLANE, part_rows, width), bf16),
             pltpu.VMEM((PLANE, held, width), bf16),
             pltpu.VMEM((PLANE, held, value_width), bf16),
-            pltpu.VMEM((value_width, tokens), bf16),
-            pltpu.VMEM((2, tokens, tile), f32),
+            pltpu.VMEM((PLANE, value_width, held), bf16),
+            pltpu.VMEM((2, tokens // HALVES, tile), f32),
             pltpu.VMEM((PARTS, RING, 2, value_width, tile), f32),
             pltpu.VMEM((PARTS, RING, 8, RING * tile), f32),
             pltpu.VMEM((PARTS, RING, value_width, tile), bf16),
@@ -439,7 +464,7 @@
         ],
         compiler_params=pltpu.CompilerParams(
             collective_id=0, has_side_effects=True, vmem_limit_bytes=60 * 1024 * 1024),
-    )(queries, keys, values, low, high, lambdas, gain, weights)
+    )(queries, keys, values, spans, lambdas, gain, weights)
 
 
 def per_device(
@@ -451,12 +476,10 @@
     by_head = lambda a: jnp.transpose(a, (1, 0, 2))
     asked = queries.reshape(COLUMN, SIDES, PARTS, share, heads_here, both_width).transpose(4, 2, 1, 0, 3, 5)
     asked = asked.reshape(heads_here, PARTS, part_rows, both_width)
-    ordered = lambda a: a.reshape(RING, PLANE, COLUMN, SIDES, PARTS, share).transpose(4, 0, 1, 3, 2, 5).reshape(1, -1)
-    low = ordered(doc_spans[:, 0] * BLK)
-    high = ordered(jnp.minimum(positions + 1, doc_spans[:, 1] * BLK))
-    gain = jnp.broadcast_to(norm_gain[:, :, None], norm_gain.shape + (128,))
+    spans = jnp.stack([doc_spans[:, 0] * BLK, jnp.minimum(positions + 1, doc_spans[:, 1] * BLK)])
+    spans = spans.reshape(2, RING, PLANE, COLUMN, SIDES, PARTS, share).transpose(0, 5, 1, 2, 4, 3, 6).reshape(2, -1)
     return layer(
-        asked, by_head(cache_keys), by_head(cache_values), low, high, lambdas, gain, out_weight)
+        asked, by_head(cache_keys), by_head(cache_values), spans, lambdas, norm_gain, out_weight)
 
 
 def solution(mesh):

time: 145 us -> 143 us (0.986)
  local copies, waits for them, and re-layouts: 11.2 us -> 8.9 us
    broadcast_in_dim x1 -> x0, local copies, waits for them, and re-layouts: 1.68 us -> none  [per_device(): gain = jnp.broadcast_to(norm_gain[:, :, None], norm_gain.shape + (128,))]
where the time goes in v3:
time: 143 us; the launch traced here: 142 us
  Pallas kernels  132 us (92%)
  local copies, waits for them, and re-layouts  8.9 us (6%)
  other arithmetic  1.75 us (1%)
    pallas_call x1, Pallas kernels, layer(): pl.pallas_call(attention_kernel, out_shape=jax.ShapeDtypeStruct((parts *...  132 us
    transpose x1, local copies, waits for them, and re-layouts, per_device(): by_head = lambda a: jnp.transpose(a, (1, 0, 2))  3.17 us

profile of v3, /device:TPU:0, one launch (start us, length us, event | category | flops | bytes accessed | tf_op | source)
XLA Modules:
  0.0 142.2 jit_solution(15458055727964865667)
XLA Ops:
  0.0 0.9 multiply_reduce_fusion
  0.9 0.7 add_minimum_fusion
  1.6 0.3 stack.7
  2.0 0.3 mul.21
  2.3 0.1 add_bitcast_fusion
  2.5 0.1 copy.16
  2.6 1.1 reshape.30.span_ref
  3.7 1.9 %copy.13 = bf16[4,2,4,8,4,256]{5,3,0,1,2,4:T(8,128)(2,1)} copy(bf16[4,2,4,8,4,256]{5,4,3,2,1,0:T(4,128)(2,1)} %bitcast.12) | data formatting | bytes 1048576 | tf_op jit(solution)/shard_map/reshape | solution.py:477
  5.7 3.2 %copy_bitcast_fusion = (bf16[4,512,256]{2,1,0:T(8,128)(2,1)}, bf16[4,512,256]{2,1,0:T(8,128)(2,1)}) fusion(bf16[512,4,256]{2,1,0:T(4,128)(2,1)} %param.10, bf16[512,4,256]{2,1,0:T(4,128)(2,1)} %param.9), kind=kLoop, calls=%fused_computation | loop fusion | bytes 4194304 | tf_op jit(solution)/shard_map/transpose | solution.py:476
  8.8 131.5 %shard_map.82 = bf16[32,8192]{1,0:T(8,128)(2,1)} custom-call(bf16[4,4,64,256]{3,2,1,0:T(8,128)(2,1)} %bitcast.11, bf16[4,512,256]{2,1,0:T(8,128)(2,1)} %get-tuple-element.8.k_ref, bf16[4,512,256]{2,1,0:T(8,128)(2,1)} %get-tuple-element.7.v_ref, s32[2,4096]{1,0:T(2,128)} %reshape.30.span_ref, f32[4]{0:T(128)} %lam_ref.1, f32[4,256]{1,0:T(4,128)} %gain_ref.1, ...), custom_call_target="tpu_custom_call" | custom-call | tf_op jit(solution)/shard_map/pallas_call | solution.py:429
  140.4 1.9 %copy.20 = bf16[32,8192]{1,0:T(8,128)(2,1)} copy(bf16[32,8192]{1,0:T(8,128)(2,1)} %shard_map.82) | data formatting | bytes 1048576

commit v4 on v3

--- a/solution.py
+++ b/solution.py
@@ -18,7 +18,7 @@
 RING = 4
 COLUMN = 4
 SIDES = 2
-HALVES = 2
+WEIGHTS_AT = 12
 PARTS = 4
 
 
@@ -40,14 +40,12 @@
     tile = PLANE * part_rows
     held = k_all.shape[1]
     tokens = PLANE * held
-    near = tokens // HALVES
     value_width = v_all.shape[2]
     half = q_all.shape[4] // 2
     step = min(256, held)
-    steps = near // step
+    steps = tokens // step
     factor = (half ** -0.5) * LOG2_E
-    half_tiles = PARTS * RING
-    n_tiles = HALVES * half_tiles
+    n_tiles = PARTS * RING
     zp = j // 2
     core = lax.rem(j, 2)
     share = part_rows // (COLUMN * SIDES)
@@ -80,9 +78,9 @@
     pl.semaphore_signal(barrier, inc=1, device_id=other_side, device_id_type=MESH)
     pl.semaphore_wait(barrier, PLANE + RING + COLUMN - 2)
 
-    def q1(d, dst):
-        return pltpu.make_async_remote_copy(
-            q_ref.at[partner(d)], q_all.at[:, x, dst], q1_send.at[d], q1_recv.at[d],
+    def q1(r, d, dst):
+        return pltpu.make_async_remote_copy(
+            q_ref.at[partner(d), r], q_all.at[r, x, dst], q1_send.at[r * PLANE + d], q1_recv.at[r * PLANE + d],
             device_id=plane_device(d), device_id_type=MESH)
 
     def k1(d, dst):
@@ -95,9 +93,11 @@
             v_ref.at[partner(d)], v_all.at[dst], v_send.at[d], v_recv.at[d],
             device_id=plane_device(d), device_id_type=MESH)
 
-    def q2(r, d, dst):
-        return pltpu.make_async_remote_copy(
-            q_all.at[r, x], q_all.at[r, dst], q2_send.at[r * RING + d], q2_recv.at[r * RING + d],
+    def q2(r, d, dst, far):
+        pair = pl.ds(2 * (1 - zp if far else zp), 2)
+        at = (r * RING + d) * 2 + far
+        return pltpu.make_async_remote_copy(
+            q_all.at[r, x, pair], q_all.at[r, dst, pair], q2_send.at[at], q2_recv.at[at],
             device_id=ring_device(RING - d), device_id_type=MESH)
 
     def st(r, d, dst):
@@ -136,70 +136,81 @@
     def ring_source(d):
         return lax.rem(x + d, RING)
 
-    for d in range(1, PLANE):
-        q1(d, j).start()
-    for d in range(1, PLANE):
-        k1(d, j).start()
-        v1(d, j).start()
+    def pass_on(r, far):
+        for d in (1, 3, 2):
+            q2(r, d, x, far).start()
+
     own_copies = [
         pltpu.make_async_copy(q_ref.at[j], q_all.at[:, x, j], local_sem.at[0]),
         pltpu.make_async_copy(k_ref.at[j], k_all.at[j], local_sem.at[1]),
         pltpu.make_async_copy(v_ref.at[j], v_all.at[j], local_sem.at[2]),
     ]
-    for copy in own_copies:
-        copy.start()
+    own_copies[0].start()
+    for d in (2, 3):
+        q1(0, d, j).start()
+    for r in range(PARTS):
+        q1(r, 1, j).start()
+    for d in (2, 3):
+        k1(d, j).start()
+        v1(d, j).start()
+    k1(1, j).start()
+    v1(1, j).start()
+    own_copies[1].start()
+    own_copies[2].start()
     weights_copy = pltpu.make_async_copy(w_ref, w_all, local_sem.at[3])
     weights_copy.start()
-    def clear(i, carry):
-        r, plane = i // RING, lax.rem(i, RING)
-        sums[r, plane] = jnp.zeros(sums.shape[2:], jnp.float32)
-        lanes = pl.ds(pl.multiple_of(plane * tile, tile), tile)
-        for m in range(2):
-            stats[r, x, 2 * m:2 * m + 1, lanes] = jnp.full((1, tile), TOP_START, jnp.float32)
-            stats[r, x, 2 * m + 1:2 * m + 2, lanes] = jnp.zeros((1, tile), jnp.float32)
-        return carry
-
-    lax.fori_loop(0, half_tiles, clear, 0)
     own_copies[0].wait()
-    for d in range(1, PLANE):
-        q1(d, partner(d)).wait_recv()
-    for r in range(PARTS):
-        for d in (1, 3, 2):
-            q2(r, d, x).start()
+    q1(0, 1, partner(1)).wait_recv()
+    pass_on(0, 0)
+    for d in (2, 3):
+        q1(0, d, partner(d)).wait_recv()
+    pass_on(0, 1)
+    for r in range(1, PARTS):
+        q1(r, 1, partner(1)).wait_recv()
+        pass_on(r, 0)
     own_copies[1].wait()
     own_copies[2].wait()
     k1(1, partner(1)).wait_recv()
     v1(1, partner(1)).wait_recv()
-    for source in (j, partner(1)):
-        v_turned[source] = v_all[source].T
+    v_turned[j] = v_all[j].T
+    v_turned[partner(1)] = v_all[partner(1)].T
+    for d in (2, 3):
+        k1(d, partner(d)).wait_recv()
+        v1(d, partner(d)).wait_recv()
+    for r in range(1, PARTS):
+        for d in (2, 3):
+            q1(r, d, j).start()
+    for d in (2, 3):
+        v_turned[partner(d)] = v_all[partner(d)].T
+
+    def far_questions(r):
+        for d in (2, 3):
+            q1(r + 1, d, partner(d)).wait_recv()
+        pass_on(r + 1, 1)
 
     def place(n):
-        late = n // half_tiles
-        at = lax.rem(n, half_tiles)
-        return 2 * (zp + late - 2 * zp * late), at // RING, lax.rem(x + lax.rem(at, RING), RING)
-
-    def score_step(n, m, t, slot, top):
-        source, r, plane = place(n)
+        return n // RING, lax.rem(x + lax.rem(n, RING), RING)
+
+    def score_step(n, m, t, top):
+        r, plane = place(n)
         query = q_all[r, plane, :, :, m * half:(m + 1) * half].reshape(tile, half)
         lanes = pl.ds(pl.multiple_of((r * RING + plane) * tile, tile), tile)
-        base = x * tokens + source * held
-        low = span_ref[0:1, lanes] - base
-        high = span_ref[1:2, lanes] - base
+        low = span_ref[0:1, lanes] - x * tokens
+        high = span_ref[1:2, lanes] - x * tokens
         first = t * step
-        key = k_all[source + first // held, first % held:first % held + step, m * half:(m + 1) * half]
+        key = k_all[first // held, first % held:first % held + step, m * half:(m + 1) * half]
         s = lax.dot_general(key, query, (((1,), (1,)), ((), ())), preferred_element_type=jnp.float32)
         at = lax.broadcasted_iota(jnp.int32, (step, tile), 0) + first
         s = jnp.where((at >= low) & (at < high), s, NEG_BIG)
-        scores[slot, first:first + step, :] = s
+        scores[m, first:first + step, :] = s
         return jnp.maximum(top, jnp.max(s, axis=0, keepdims=True))
 
-    def weight_step(n, t, slot, shift, total, summed):
-        source, _, _ = place(n)
+    def weight_step(m, t, shift, total, summed):
         first = t * step
-        w = jnp.exp2(scores[slot, first:first + step, :] * factor - shift)
+        w = jnp.exp2(scores[m, first:first + step, :] * factor - shift)
         total = total + jnp.sum(w, axis=0, keepdims=True)
         part = jnp.dot(
-            v_turned[source + first // held, :, first % held:first % held + step], w.astype(jnp.bfloat16),
+            v_turned[first // held, :, first % held:first % held + step], w.astype(jnp.bfloat16),
             preferred_element_type=jnp.float32)
         return total, (part if summed is None else summed + part)
 
@@ -211,6 +222,7 @@
         for d in range(1, RING):
             st(r, d, ring_source(d)).wait_recv()
         lam = lam_ref[j]
+        kept = lax.rem(r, 2)
         for d in (1, 3, 2, 0):
             plane = lax.rem(x + RING - d, RING)
             lanes = pl.ds(pl.multiple_of(plane * tile, tile), tile)
@@ -222,7 +234,7 @@
                 total = sum(a * jnp.exp2((b - top) * factor) for a, b in zip(totals, tops))
                 own_top = stats[r, x, 2 * m:2 * m + 1, lanes]
                 shares.append(jnp.exp2((own_top - top) * factor) / total)
-            piece = sums[r, plane, 0] * shares[0] - sums[r, plane, 1] * (shares[1] * lam)
+            piece = sums[kept, plane, 0] * shares[0] - sums[kept, plane, 1] * (shares[1] * lam)
             if d == 0:
                 own_piece[r] = piece
             else:
@@ -330,54 +342,50 @@
 
         lax.fori_loop(0, fold // stripe, last_stripe, 0)
 
-    stages = ((send_stats, 19), (combine, 23), (finish, 32), (project, 34), (add_first, 45), (add_last, 53))
+    stages = ((send_stats, 3), (combine, 5), (finish, 11), (project, 14), (add_first, 20), (add_last, 24))
 
     def run_stages(n):
         for stage, lag in reversed(stages):
-            @pl.when((n >= lag) & (n < lag + PARTS * RING) & (lax.rem(n + 16 * RING - lag, RING) == 0))
+            @pl.when((n >= lag) & (n < lag + n_tiles) & (lax.rem(n + 16 * RING - lag, RING) == 0))
             def _():
                 stage((n - lag) // RING)
 
-    def start_top(n, m):
-        _, r, plane = place(n)
-        return stats[r, x, 2 * m:2 * m + 1, pl.ds(pl.multiple_of(plane * tile, tile), tile)]
-
-    top = start_top(0, 0)
+    first_top = jnp.full((1, tile), TOP_START, jnp.float32)
+    top = first_top
     for t in range(steps):
-        top = score_step(0, 0, t, 0, top)
+        top = score_step(0, 0, t, top)
 
     def body(n, top):
-        _, r, plane = place(n)
+        r, plane = place(n)
         later = jnp.minimum(n + 1, n_tiles - 1)
-        later_d = lax.rem(later, RING)
-
-        @pl.when((n + 1 < half_tiles) & (later_d > 0))
+        later_r, later_d = later // RING, lax.rem(later, RING)
+
+        @pl.when((lax.rem(n, RING) == 1) & (r + 1 < PARTS))
         def _():
-            q2(later // RING, later_d, ring_source(later_d)).wait_recv()
-
-        @pl.when(n + 1 == half_tiles)
+            far_questions(r)
+
+        @pl.when((n + 1 < n_tiles) & (later_d > 0))
         def _():
-            for d in (2, 3):
-                k1(d, partner(d)).wait_recv()
-                v1(d, partner(d)).wait_recv()
-                v_turned[partner(d)] = v_all[partner(d)].T
-            weights_copy.wait()
+            for far in range(2):
+                q2(later_r, later_d, ring_source(later_d), far).wait_recv()
 
         lanes = pl.ds(pl.multiple_of(plane * tile, tile), tile)
         for m in range(2):
-            following = n if m == 0 else later
-            next_top = start_top(following, 1 - m)
+            next_top = first_top
             total = jnp.zeros((1, tile), jnp.float32)
             summed = None
             shift = top * factor
             for t in range(steps):
-                next_top = score_step(following, 1 - m, t, 1 - m, next_top)
-                total, summed = weight_step(n, t, m, shift, total, summed)
-            kept = jnp.exp2((stats[r, x, 2 * m:2 * m + 1, lanes] - top) * factor)
-            sums[r, plane, m] = sums[r, plane, m] * kept + summed
+                next_top = score_step(n if m == 0 else later, 1 - m, t, next_top)
+                total, summed = weight_step(m, t, shift, total, summed)
+            sums[lax.rem(r, 2), plane, m] = summed
             stats[r, x, 2 * m:2 * m + 1, lanes] = top
-            stats[r, x, 2 * m + 1:2 * m + 2, lanes] = stats[r, x, 2 * m + 1:2 * m + 2, lanes] * kept + total
+            stats[r, x, 2 * m + 1:2 * m + 2, lanes] = total
             top = next_top
+
+        @pl.when(n == WEIGHTS_AT)
+        def _():
+            weights_copy.wait()
 
         run_stages(n)
         return top
@@ -388,13 +396,15 @@
         run_stages(n)
         return carry
 
-    lax.fori_loop(n_tiles, stages[-1][1] + PARTS * RING, tail, 0)
+    lax.fori_loop(n_tiles, stages[-1][1] + n_tiles - RING + 1, tail, 0)
 
     def last_waits(r, carry):
         for d in range(1, PLANE):
             n1(r, d, j).wait_send()
+            q1(r, d, j).wait_send()
         for d in range(1, RING):
-            q2(r, d, x).wait_send()
+            q2(r, d, x, 0).wait_send()
+            q2(r, d, x, 1).wait_send()
             st(r, d, x).wait_send()
             o1(r, d, d).wait_send()
         for d in range(1, COLUMN):
@@ -406,7 +416,6 @@
 
     lax.fori_loop(0, PARTS, last_waits, 0)
     for d in range(1, PLANE):
-        q1(d, j).wait_send()
         k1(d, j).wait_send()
         v1(d, j).wait_send()
     for i in range(columns // stripe):
@@ -436,8 +445,8 @@
             pltpu.VMEM((PLANE, held, width), bf16),
             pltpu.VMEM((PLANE, held, value_width), bf16),
             pltpu.VMEM((PLANE, value_width, held), bf16),
-            pltpu.VMEM((2, tokens // HALVES, tile), f32),
-            pltpu.VMEM((PARTS, RING, 2, value_width, tile), f32),
+            pltpu.VMEM((2, tokens, tile), f32),
+            pltpu.VMEM((2, RING, 2, value_width, tile), f32),
             pltpu.VMEM((PARTS, RING, 8, RING * tile), f32),
             pltpu.VMEM((PARTS, RING, value_width, tile), bf16),
             pltpu.VMEM((PARTS, RING, value_width, tile), bf16),
@@ -455,8 +464,8 @@
             pltpu.VMEM((PARTS, COLUMN, 2 * share, area // 2), bf16),
             pltpu.VMEM((PARTS, COLUMN, 2 * share, area // 2), bf16),
             pltpu.VMEM((PARTS, share, columns), f32),
-            dma((PLANE,)), dma((PLANE,)), dma((PLANE,)), dma((PLANE,)), dma((PLANE,)), dma((PLANE,)),
-            dma((PARTS * RING,)), dma((PARTS * RING,)), dma((PARTS * RING,)), dma((PARTS * RING,)),
+            dma((PARTS * PLANE,)), dma((PARTS * PLANE,)), dma((PLANE,)), dma((PLANE,)), dma((PLANE,)), dma((PLANE,)),
+            dma((2 * PARTS * RING,)), dma((2 * PARTS * RING,)), dma((PARTS * RING,)), dma((PARTS * RING,)),
             dma((PARTS * RING,)), dma((PARTS * RING,)), dma((PARTS * PLANE,)), dma((PARTS * PLANE,)),
             dma((4,)),
             dma((PARTS * COLUMN,)), dma((PARTS * COLUMN,)), dma((PARTS,)), dma((PARTS,)),

time: 143 us -> 138 us (0.965)
  Pallas kernels: 132 us -> 127 us
    pallas_call x1, Pallas kernels: 132 us -> 127 us  [layer(): pl.pallas_call(attention_kernel, out_shape=jax.ShapeDtypeStruct((parts *...]
where the time goes in v4:
time: 138 us
  Pallas kernels  127 us (92%)
  local copies, waits for them, and re-layouts  8.9 us (6%)
  other arithmetic  1.75 us (1%)
    pallas_call x1, Pallas kernels, layer(): pl.pallas_call(attention_kernel, out_shape=jax.ShapeDtypeStruct((parts *...  127 us
    transpose x1, local copies, waits for them, and re-layouts, per_device(): by_head = lambda a: jnp.transpose(a, (1, 0, 2))  3.17 us

profile of v4, /device:TPU:0, one launch (start us, length us, event | category | flops | bytes accessed | tf_op | source)
XLA Modules:
  0.0 137.9 jit_solution(15755505043275433336)
XLA Ops:
  0.0 0.9 multiply_reduce_fusion
  0.9 0.7 add_minimum_fusion
  1.6 0.3 stack.7
  2.0 0.3 mul.21
  2.3 0.1 add_bitcast_fusion
  2.5 0.1 copy.16
  2.6 1.1 reshape.30.span_ref
  3.7 1.9 %copy.13 = bf16[4,2,4,8,4,256]{5,3,0,1,2,4:T(8,128)(2,1)} copy(bf16[4,2,4,8,4,256]{5,4,3,2,1,0:T(4,128)(2,1)} %bitcast.12) | data formatting | bytes 1048576 | tf_op jit(solution)/shard_map/reshape | solution.py:486
  5.7 3.2 %copy_bitcast_fusion = (bf16[4,512,256]{2,1,0:T(8,128)(2,1)}, bf16[4,512,256]{2,1,0:T(8,128)(2,1)}) fusion(bf16[512,4,256]{2,1,0:T(4,128)(2,1)} %param.10, bf16[512,4,256]{2,1,0:T(4,128)(2,1)} %param.9), kind=kLoop, calls=%fused_computation | loop fusion | bytes 4194304 | tf_op jit(solution)/shard_map/transpose | solution.py:485
  8.8 127.2 %shard_map.82 = bf16[32,8192]{1,0:T(8,128)(2,1)} custom-call(bf16[4,4,64,256]{3,2,1,0:T(8,128)(2,1)} %bitcast.11, bf16[4,512,256]{2,1,0:T(8,128)(2,1)} %get-tuple-element.8.k_ref, bf16[4,512,256]{2,1,0:T(8,128)(2,1)} %get-tuple-element.7.v_ref, s32[2,4096]{1,0:T(2,128)} %reshape.30.span_ref, f32[4]{0:T(128)} %lam_ref.1, f32[4,256]{1,0:T(4,128)} %gain_ref.1, ...), custom_call_target="tpu_custom_call" | custom-call | tf_op jit(solution)/shard_map/pallas_call | solution.py:438
  136.0 1.9 %copy.20 = bf16[32,8192]{1,0:T(8,128)(2,1)} copy(bf16[32,8192]{1,0:T(8,128)(2,1)} %shard_map.82) | data formatting | bytes 1048576

commit v5 on v3

--- a/solution.py
+++ b/solution.py
@@ -55,6 +55,7 @@
     area = columns // 2
     fold = area // 2
     stripe = min(512, fold)
+    wide = min(2048, area)
 
     def partner(k):
         return (2 * zp + 1 - core, 2 * (1 - zp) + core, PLANE - 1 - j)[k - 1]
@@ -95,9 +96,11 @@
             v_ref.at[partner(d)], v_all.at[dst], v_send.at[d], v_recv.at[d],
             device_id=plane_device(d), device_id_type=MESH)
 
-    def q2(r, d, dst):
-        return pltpu.make_async_remote_copy(
-            q_all.at[r, x], q_all.at[r, dst], q2_send.at[r * RING + d], q2_recv.at[r * RING + d],
+    def q2(r, d, dst, far):
+        pair = pl.ds(2 * (1 - zp if far else zp), 2)
+        at = (r * RING + d) * 2 + far
+        return pltpu.make_async_remote_copy(
+            q_all.at[r, x, pair], q_all.at[r, dst, pair], q2_send.at[at], q2_recv.at[at],
             device_id=ring_device(RING - d), device_id_type=MESH)
 
     def st(r, d, dst):
@@ -136,20 +139,30 @@
     def ring_source(d):
         return lax.rem(x + d, RING)
 
-    for d in range(1, PLANE):
-        q1(d, j).start()
-    for d in range(1, PLANE):
-        k1(d, j).start()
-        v1(d, j).start()
+    def pass_on(r, far):
+        for d in (1, 3, 2):
+            q2(r, d, x, far).start()
+
     own_copies = [
         pltpu.make_async_copy(q_ref.at[j], q_all.at[:, x, j], local_sem.at[0]),
         pltpu.make_async_copy(k_ref.at[j], k_all.at[j], local_sem.at[1]),
         pltpu.make_async_copy(v_ref.at[j], v_all.at[j], local_sem.at[2]),
     ]
-    for copy in own_copies:
-        copy.start()
+    own_copies[0].start()
+    for d in (1, 2, 3):
+        q1(d, j).start()
+    for d in (2, 3, 1):
+        k1(d, j).start()
+        v1(d, j).start()
+    own_copies[1].start()
+    own_copies[2].start()
     weights_copy = pltpu.make_async_copy(w_ref, w_all, local_sem.at[3])
     weights_copy.start()
+    own_copies[0].wait()
+    q1(1, partner(1)).wait_recv()
+    pass_on(0, 0)
+    pass_on(1, 0)
+
     def clear(i, carry):
         r, plane = i // RING, lax.rem(i, RING)
         sums[r, plane] = jnp.zeros(sums.shape[2:], jnp.float32)
@@ -160,12 +173,13 @@
         return carry
 
     lax.fori_loop(0, half_tiles, clear, 0)
-    own_copies[0].wait()
-    for d in range(1, PLANE):
+    for d in (2, 3):
         q1(d, partner(d)).wait_recv()
-    for r in range(PARTS):
-        for d in (1, 3, 2):
-            q2(r, d, x).start()
+    pass_on(0, 1)
+    pass_on(1, 1)
+    for r in range(2, PARTS):
+        pass_on(r, 0)
+        pass_on(r, 1)
     own_copies[1].wait()
     own_copies[2].wait()
     k1(1, partner(1)).wait_recv()
@@ -249,27 +263,27 @@
         rows = jnp.concatenate([normed[h, r] for h in range(PLANE)], axis=1)
 
         def product(first):
-            return jnp.dot(rows, w_all[:, pl.ds(pl.multiple_of(first, stripe), stripe)], preferred_element_type=jnp.float32)
-
-        def b_stripe(i, carry):
-            at = pl.ds(pl.multiple_of(i * stripe, stripe), stripe)
-            got = product(area + i * stripe).astype(jnp.bfloat16)
+            return jnp.dot(rows, w_all[:, pl.ds(pl.multiple_of(first, wide), wide)], preferred_element_type=jnp.float32)
+
+        def b_wide(i, carry):
+            at = pl.ds(pl.multiple_of(i * wide, wide), wide)
+            got = product(area + i * wide).astype(jnp.bfloat16)
             for side_to in range(SIDES):
                 b_out[r, side_to, :, at] = got[side_to * COLUMN * share:(side_to + 1) * COLUMN * share]
             return carry
 
-        def a_stripe(i, carry):
-            at = pl.ds(pl.multiple_of(i * stripe, stripe), stripe)
-            got = product(i * stripe)
+        def a_wide(i, carry):
+            at = pl.ds(pl.multiple_of(i * wide, wide), wide)
+            got = product(i * wide)
             for y_to in range(COLUMN):
                 a_out[r, y_to, :, at] = jnp.concatenate(
                     [got[(s * COLUMN + y_to) * share:(s * COLUMN + y_to + 1) * share] for s in range(SIDES)], axis=0
                 ).astype(jnp.bfloat16)
             return carry
 
-        lax.fori_loop(0, area // stripe, b_stripe, 0)
+        lax.fori_loop(0, area // wide, b_wide, 0)
         b1(r).start()
-        lax.fori_loop(0, area // stripe, a_stripe, 0)
+        lax.fori_loop(0, area // wide, a_wide, 0)
         for d in (1, 3, 2):
             a1(r, d).start()
 
@@ -330,7 +344,7 @@
 
         lax.fori_loop(0, fold // stripe, last_stripe, 0)
 
-    stages = ((send_stats, 19), (combine, 23), (finish, 32), (project, 34), (add_first, 45), (add_last, 53))
+    stages = ((send_stats, 19), (combine, 24), (finish, 33), (project, 36), (add_first, 41), (add_last, 50))
 
     def run_stages(n):
         for stage, lag in reversed(stages):
@@ -353,7 +367,8 @@
 
         @pl.when((n + 1 < half_tiles) & (later_d > 0))
         def _():
-            q2(later // RING, later_d, ring_source(later_d)).wait_recv()
+            for far in range(2):
+                q2(later // RING, later_d, ring_source(later_d), far).wait_recv()
 
         @pl.when(n + 1 == half_tiles)
         def _():
@@ -394,7 +409,8 @@
         for d in range(1, PLANE):
             n1(r, d, j).wait_send()
         for d in range(1, RING):
-            q2(r, d, x).wait_send()
+            q2(r, d, x, 0).wait_send()
+            q2(r, d, x, 1).wait_send()
             st(r, d, x).wait_send()
             o1(r, d, d).wait_send()
         for d in range(1, COLUMN):
@@ -456,7 +472,7 @@
             pltpu.VMEM((PARTS, COLUMN, 2 * share, area // 2), bf16),
             pltpu.VMEM((PARTS, share, columns), f32),
             dma((PLANE,)), dma((PLANE,)), dma((PLANE,)), dma((PLANE,)), dma((PLANE,)), dma((PLANE,)),
-            dma((PARTS * RING,)), dma((PARTS * RING,)), dma((PARTS * RING,)), dma((PARTS * RING,)),
+            dma((2 * PARTS * RING,)), dma((2 * PARTS * RING,)), dma((PARTS * RING,)), dma((PARTS * RING,)),
             dma((PARTS * RING,)), dma((PARTS * RING,)), dma((PARTS * PLANE,)), dma((PARTS * PLANE,)),
             dma((4,)),
             dma((PARTS * COLUMN,)), dma((PARTS * COLUMN,)), dma((PARTS,)), dma((PARTS,)),

time: 143 us -> 130 us (0.909)
  Pallas kernels: 132 us -> 118 us
    pallas_call x1, Pallas kernels: 132 us -> 118 us  [layer(): pl.pallas_call(attention_kernel, out_shape=jax.ShapeDtypeStruct((parts *...]
where the time goes in v5:
time: 130 us; the launch traced here: 129 us
  Pallas kernels  118 us (91%)
  local copies, waits for them, and re-layouts  8.9 us (7%)
  other arithmetic  1.75 us (1%)
    pallas_call x1, Pallas kernels, layer(): pl.pallas_call(attention_kernel, out_shape=jax.ShapeDtypeStruct((parts *...  118 us
    transpose x1, local copies, waits for them, and re-layouts, per_device(): by_head = lambda a: jnp.transpose(a, (1, 0, 2))  3.17 us

profile of v5, /device:TPU:0, one launch (start us, length us, event | category | flops | bytes accessed | tf_op | source)
XLA Modules:
  0.0 128.7 jit_solution(17809070084150306004)
XLA Ops:
  0.0 0.9 multiply_reduce_fusion
  0.9 0.7 add_minimum_fusion
  1.6 0.3 stack.7
  2.0 0.3 mul.21
  2.3 0.1 add_bitcast_fusion
  2.5 0.1 copy.16
  2.6 1.1 reshape.30.span_ref
  3.7 1.9 %copy.13 = bf16[4,2,4,8,4,256]{5,3,0,1,2,4:T(8,128)(2,1)} copy(bf16[4,2,4,8,4,256]{5,4,3,2,1,0:T(4,128)(2,1)} %bitcast.12) | data formatting | bytes 1048576 | tf_op jit(solution)/shard_map/reshape | solution.py:493
  5.7 3.2 %copy_bitcast_fusion = (bf16[4,512,256]{2,1,0:T(8,128)(2,1)}, bf16[4,512,256]{2,1,0:T(8,128)(2,1)}) fusion(bf16[512,4,256]{2,1,0:T(4,128)(2,1)} %param.10, bf16[512,4,256]{2,1,0:T(4,128)(2,1)} %param.9), kind=kLoop, calls=%fused_computation | loop fusion | bytes 4194304 | tf_op jit(solution)/shard_map/transpose | solution.py:492
  8.8 118.0 %shard_map.82 = bf16[32,8192]{1,0:T(8,128)(2,1)} custom-call(bf16[4,4,64,256]{3,2,1,0:T(8,128)(2,1)} %bitcast.11, bf16[4,512,256]{2,1,0:T(8,128)(2,1)} %get-tuple-element.8.k_ref, bf16[4,512,256]{2,1,0:T(8,128)(2,1)} %get-tuple-element.7.v_ref, s32[2,4096]{1,0:T(2,128)} %reshape.30.span_ref, f32[4]{0:T(128)} %lam_ref.1, f32[4,256]{1,0:T(4,128)} %gain_ref.1, ...), custom_call_target="tpu_custom_call" | custom-call | tf_op jit(solution)/shard_map/pallas_call | solution.py:445
  126.8 1.9 %copy.20 = bf16[32,8192]{1,0:T(8,128)(2,1)} copy(bf16[32,8192]{1,0:T(8,128)(2,1)} %shard_map.82) | data formatting | bytes 1048576

commit v6 on v5

--- a/solution.py
+++ b/solution.py
@@ -344,7 +344,7 @@
 
         lax.fori_loop(0, fold // stripe, last_stripe, 0)
 
-    stages = ((send_stats, 19), (combine, 24), (finish, 33), (project, 36), (add_first, 41), (add_last, 50))
+    stages = ((send_stats, 19), (combine, 24), (finish, 32), (project, 36), (add_first, 39), (add_last, 45))
 
     def run_stages(n):
         for stage, lag in reversed(stages):

time: 130 us -> 126 us (0.969)
  Pallas kernels: 118 us -> 114 us
    pallas_call x1, Pallas kernels: 118 us -> 114 us  [layer(): pl.pallas_call(attention_kernel, out_shape=jax.ShapeDtypeStruct((parts *...]
where the time goes in v6:
time: 126 us; the launch traced here: 125 us
  Pallas kernels  114 us (90%)
  local copies, waits for them, and re-layouts  8.9 us (7%)
  other arithmetic  1.75 us (1%)
    pallas_call x1, Pallas kernels, layer(): pl.pallas_call(attention_kernel, out_shape=jax.ShapeDtypeStruct((parts *...  114 us
    transpose x1, local copies, waits for them, and re-layouts, per_device(): by_head = lambda a: jnp.transpose(a, (1, 0, 2))  3.17 us

profile of v6, /device:TPU:0, one launch (start us, length us, event | category | flops | bytes accessed | tf_op | source)
XLA Modules:
  0.0 124.5 jit_solution(7652979139838337897)
XLA Ops:
  0.0 0.9 multiply_reduce_fusion
  0.9 0.7 add_minimum_fusion
  1.6 0.3 stack.7
  2.0 0.3 mul.21
  2.3 0.1 add_bitcast_fusion
  2.5 0.1 copy.16
  2.6 1.1 reshape.30.span_ref
  3.7 1.9 %copy.13 = bf16[4,2,4,8,4,256]{5,3,0,1,2,4:T(8,128)(2,1)} copy(bf16[4,2,4,8,4,256]{5,4,3,2,1,0:T(4,128)(2,1)} %bitcast.12) | data formatting | bytes 1048576 | tf_op jit(solution)/shard_map/reshape | solution.py:493
  5.7 3.2 %copy_bitcast_fusion = (bf16[4,512,256]{2,1,0:T(8,128)(2,1)}, bf16[4,512,256]{2,1,0:T(8,128)(2,1)}) fusion(bf16[512,4,256]{2,1,0:T(4,128)(2,1)} %param.10, bf16[512,4,256]{2,1,0:T(4,128)(2,1)} %param.9), kind=kLoop, calls=%fused_computation | loop fusion | bytes 4194304 | tf_op jit(solution)/shard_map/transpose | solution.py:492
  8.8 113.8 %shard_map.82 = bf16[32,8192]{1,0:T(8,128)(2,1)} custom-call(bf16[4,4,64,256]{3,2,1,0:T(8,128)(2,1)} %bitcast.11, bf16[4,512,256]{2,1,0:T(8,128)(2,1)} %get-tuple-element.8.k_ref, bf16[4,512,256]{2,1,0:T(8,128)(2,1)} %get-tuple-element.7.v_ref, s32[2,4096]{1,0:T(2,128)} %reshape.30.span_ref, f32[4]{0:T(128)} %lam_ref.1, f32[4,256]{1,0:T(4,128)} %gain_ref.1, ...), custom_call_target="tpu_custom_call" | custom-call | tf_op jit(solution)/shard_map/pallas_call | solution.py:445
  122.7 1.9 %copy.20 = bf16[32,8192]{1,0:T(8,128)(2,1)} copy(bf16[32,8192]{1,0:T(8,128)(2,1)} %shard_map.82) | data formatting | bytes 1048576

commit v7 on v6

--- a/solution.py
+++ b/solution.py
@@ -151,7 +151,7 @@
     own_copies[0].start()
     for d in (1, 2, 3):
         q1(d, j).start()
-    for d in (2, 3, 1):
+    for d in (1, 2, 3):
         k1(d, j).start()
         v1(d, j).start()
     own_copies[1].start()

time: 126 us -> 126 us (level)
  no operation moved by 1% of the time
where the time goes in v7:
time: 126 us; the launch traced here: 125 us
  Pallas kernels  114 us (90%)
  local copies, waits for them, and re-layouts  8.9 us (7%)
  other arithmetic  1.75 us (1%)
    pallas_call x1, Pallas kernels, layer(): pl.pallas_call(attention_kernel, out_shape=jax.ShapeDtypeStruct((parts *...  114 us
    transpose x1, local copies, waits for them, and re-layouts, per_device(): by_head = lambda a: jnp.transpose(a, (1, 0, 2))  3.17 us

profile of v7, /device:TPU:0, one launch (start us, length us, event | category | flops | bytes accessed | tf_op | source)
XLA Modules:
  0.0 124.5 jit_solution(13030273664976406671)
XLA Ops:
  0.0 0.9 multiply_reduce_fusion
  0.9 0.7 add_minimum_fusion
  1.6 0.3 stack.7
  2.0 0.3 mul.21
  2.3 0.1 add_bitcast_fusion
  2.5 0.1 copy.16
  2.6 1.1 reshape.30.span_ref
  3.7 1.9 %copy.13 = bf16[4,2,4,8,4,256]{5,3,0,1,2,4:T(8,128)(2,1)} copy(bf16[4,2,4,8,4,256]{5,4,3,2,1,0:T(4,128)(2,1)} %bitcast.12) | data formatting | bytes 1048576 | tf_op jit(solution)/shard_map/reshape | solution.py:493
  5.7 3.2 %copy_bitcast_fusion = (bf16[4,512,256]{2,1,0:T(8,128)(2,1)}, bf16[4,512,256]{2,1,0:T(8,128)(2,1)}) fusion(bf16[512,4,256]{2,1,0:T(4,128)(2,1)} %param.10, bf16[512,4,256]{2,1,0:T(4,128)(2,1)} %param.9), kind=kLoop, calls=%fused_computation | loop fusion | bytes 4194304 | tf_op jit(solution)/shard_map/transpose | solution.py:492
  8.8 113.8 %shard_map.82 = bf16[32,8192]{1,0:T(8,128)(2,1)} custom-call(bf16[4,4,64,256]{3,2,1,0:T(8,128)(2,1)} %bitcast.11, bf16[4,512,256]{2,1,0:T(8,128)(2,1)} %get-tuple-element.8.k_ref, bf16[4,512,256]{2,1,0:T(8,128)(2,1)} %get-tuple-element.7.v_ref, s32[2,4096]{1,0:T(2,128)} %reshape.30.span_ref, f32[4]{0:T(128)} %lam_ref.1, f32[4,256]{1,0:T(4,128)} %gain_ref.1, ...), custom_call_target="tpu_custom_call" | custom-call | tf_op jit(solution)/shard_map/pallas_call | solution.py:445
  122.6 1.9 %copy.20 = bf16[32,8192]{1,0:T(8,128)(2,1)} copy(bf16[32,8192]{1,0:T(8,128)(2,1)} %shard_map.82) | data formatting | bytes 1048576
